TPU v7x, 128 devices: a whole 4x4x4 slice. The times are simulated.
128 devices in a mesh: row: 16 (over x, z_hi, core), col: 8 (over y, z_lo).
Axes of the slice: x: 4, y: 4, z: 4 (z_hi: 2, z_lo: 2; z = z_hi * 2 + z_lo), core: 2. Of those that a mesh axis runs over, the one named last changes fastest.
Arguments:
- waveform: bfloat16 [128, 1024, 8192], P(('row', 'col')), may hold values from -50 to 50, as said below
- valid_mask: int32 [128, 1024], P(('row', 'col')), may hold values 0 or 1
- band_starts: int32 [10], replicated, may hold values from 0 to 4080
- station_map: int32 [1024], replicated, may hold values from 0 to 1023, each once
Outputs:
- stacked: bfloat16 [2, 160, 1024, 1024], P(None, None, 'row', 'col')
Inputs may be any that keep to these rules, and one draw needn't show every extreme that they name: `waveform`: entries are real samples whose per-trace scale varies from trace to trace. `band_starts`: each band's 16 bins lie below 4096. `station_map`: a permutation of the stations.
All inputs are finite; a program needn't handle non-finite values. No bound on the sum of `valid_mask` on one device may be relied on, other than what follows from the above.
Results may differ from a plain program's by a relative error of at most 0.0068.
Values may be sent and summed in bfloat16 or wider, within the bound.
No kernel may reach another device: no remote copies, remote signals or barrier semaphores. Data moves between devices by JAX's collectives and lax.ppermute only.
A program may use at most 128 MiB of HBM per device.

v0:
```python
import math

import jax
import jax.numpy as jnp
from jax import lax
from jax.sharding import PartitionSpec as P

BINS = 16


def make_table(band_starts, length, bin_count):
    frequency = (band_starts[:, None] + jnp.arange(bin_count, dtype=jnp.int32)[None, :]).reshape(-1)
    samples = jnp.arange(length, dtype=jnp.int32)
    phase_index = frequency[:, None] * samples[None, :] % length
    angles = phase_index.astype(jnp.float32) * jnp.float32(2.0 * math.pi / length)
    scaling = jnp.float32(length ** (-0.5))
    return (jnp.concatenate([jnp.cos(angles), -jnp.sin(angles)], axis=0) * scaling).astype(
        jnp.bfloat16
    )


def whiten(spectra, mask_rows, band_count):
    count, double_bins, stations = spectra.shape
    half = double_bins // 2
    real_part = spectra[:, :half]
    imag_part = spectra[:, half:]
    power_bins = real_part * real_part + imag_part * imag_part
    band_mean = power_bins.reshape(count, band_count, half // band_count, stations).mean(
        axis=2, keepdims=True
    )
    band_mean = jnp.broadcast_to(
        band_mean, (count, band_count, half // band_count, stations)
    ).reshape(count, half, stations)
    factor = mask_rows[:, None, :].astype(jnp.float32) / jnp.sqrt(power_bins + band_mean + 0.1)
    return jnp.concatenate([real_part * factor, imag_part * factor], axis=1).astype(jnp.bfloat16)


def pair_product(left, right):
    return jnp.einsum("wfa,wfb->fab", left, right, preferred_element_type=jnp.float32)


def cross_spectra(left, right):
    half = left.shape[1] // 2
    real_left, imag_left = (left[:, :half], left[:, half:])
    real_right, imag_right = (right[:, :half], right[:, half:])
    real_out = pair_product(real_left, real_right) + pair_product(imag_left, imag_right)
    imag_out = pair_product(real_left, imag_right) - pair_product(imag_left, real_right)
    return jnp.stack([real_out, imag_out], axis=0)


def body(waveform, valid_mask, band_starts, station_map):
    length = waveform.shape[2]
    dft_table = make_table(band_starts, length, BINS)
    spectra = jnp.einsum("fl,wsl->wfs", dft_table, waveform, preferred_element_type=jnp.float32)
    sum_squares = jnp.einsum("wsl,wsl->ws", waveform, waveform, preferred_element_type=jnp.float32)
    rms_value = jnp.sqrt(sum_squares / length + 1e-06)
    spectra = spectra / rms_value[:, None, :]
    whitened = whiten(spectra, valid_mask, band_starts.shape[0])
    row_count = lax.axis_size("row")
    col_count = lax.axis_size("col")
    stations = whitened.shape[2]
    shard_width = stations // (row_count * col_count)
    positions = jnp.arange(stations, dtype=jnp.int32)
    shard_number = positions // shard_width
    offset_inside = positions % shard_width
    col_order = (
        shard_number % col_count * (stations // col_count)
        + shard_number // col_count * shard_width
        + offset_inside
    )
    row_source = jnp.take(whitened, station_map, axis=2)
    col_source = jnp.take(whitened, jnp.take(station_map, col_order), axis=2)
    row_local, col_local = (
        lax.all_to_all(row_source, ("row", "col"), split_axis=2, concat_axis=0, tiled=True),
        lax.all_to_all(col_source, ("row", "col"), split_axis=2, concat_axis=0, tiled=True),
    )
    row_block = lax.all_gather(row_local, "col", axis=2, tiled=True)
    scaling = jnp.float32(float(row_block.shape[0]) ** (-0.5))
    col_block = lax.all_gather(col_local, "row", axis=2, tiled=True)
    stacked = cross_spectra(row_block, col_block)
    return (stacked * scaling).astype(jnp.bfloat16)


def solution(mesh):
    placed = (P(("row", "col"), None, None), P(("row", "col"), None), P(), P())
    return jax.shard_map(
        body, mesh=mesh, in_specs=placed, out_specs=P(None, None, "row", "col"), check_vma=False
    )
```

profile of v0, /device:TPU:15, one launch (start us, length us, event | category | flops | bytes accessed | tf_op | source)
XLA Modules:
  0.0 327.4 jit_solution(16416635055304094497)
XLA Ops:
  7.3 7.2 %fusion = f32[1024]{0:T(1024)S(1)} fusion(bf16[1,1024,8192]{2,1,0:T(8,128)(2,1)} %param.6), kind=kLoop, calls=%fused_computation.4 | loop fusion | flops 25164800 | bytes 16781312 | tf_op jit(solution)/shard_map/wsl,wsl->ws/dot_general | solution.py:55
  14.5 4.5 %gather_fusion = s32[1024]{0:T(1024)S(1)} fusion(s32[1024]{0:T(1024)S(1)} %copy-done.1, s32[1024]{0:T(1024)S(1)} %broadcast_clamp_fusion.1), kind=kCustom, calls=%fused_computation.2 | custom fusion | bytes 12288 | tf_op jit(solution)/shard_map/jit(_take)/gather | solution.py:72
  19.2 23.5 %fusion.25 = (f32[160,8192]{1,0:T(8,128)}, f32[160,8192]{1,0:T(8,128)}) fusion(s32[160]{0:T(256)S(1)} %add.158), kind=kLoop, calls=%fused_computation.36 | loop fusion | flops 19660800 | bytes 10486400 | tf_op jit(solution)/shard_map/cos | solution.py:17
  42.8 12.2 %divide_bitcast_fusion = f32[1,320,1024]{2,1,0:T(8,128)S(1)} fusion(bf16[1,1024,8192]{2,1,0:T(8,128)(2,1)} %param.6, f32[160,8192]{1,0:T(8,128)} %get-tuple-element.11, f32[160,8192]{1,0:T(8,128)} %get-tuple-element.10, f32[1024]{0:T(1024)S(1)} %add_sqrt_fusion), kind=kOutput, calls=%fused_computation.38 | convolution fusion | flops 5376901120 | bytes 28577792 | tf_op jit(solution)/shard_map/fl,wsl->wfs/dot_general | solution.py:54
  56.0 4.1 %gather_fusion.2 = bf16[1024,320]{1,0:T(8,128)(2,1)S(1)} fusion(bf16[320,1024]{0,1:T(8,128)(2,1)S(1)} %copy.12, s32[1024]{0:T(1024)S(1)} %broadcast_clamp_fusion), kind=kCustom, calls=%fused_computation.1.clone | custom fusion | bytes 1314816 | tf_op jit(solution)/shard_map/jit(_take)/gather | solution.py:72
  62.1 5.9 %reduce.4 = bf16[1024,320]{1,0:T(8,128)(2,1)S(1)} reduce(bf16[1024,1,320]{2,1,0:T(2,128)(2,1)S(1)} %bitcast.92, bf16[]{:T(256)} %broadcast.314), dimensions={1}, to_apply=%bitcast.85.reduce_sub_computation | reduce | bytes 1310722
  68.8 22.6 %all_to_all.36 = bf16[128,2,1280]{2,1,0:T(2,128)(2,1)S(1)} all-to-all(bf16[128,2,1280]{2,1,0:T(2,128)(2,1)S(1)} %reshape.302), channel_id=1, replica_groups=mesh['row'=16,'col'=8] {'row','col'}, dimensions={0} | all-to-all | bytes 1310720 | tf_op jit(solution)/shard_map/all_to_all | solution.py:75
  92.9 1.3 copy.17
  94.3 4.1 %gather_fusion.1 = bf16[1024,320]{1,0:T(8,128)(2,1)S(1)} fusion(bf16[320,1024]{0,1:T(8,128)(2,1)S(1)} %copy.12, s32[1024]{0:T(1024)S(1)} %fusion.67), kind=kCustom, calls=%fused_computation.clone | custom fusion | bytes 1314816 | tf_op jit(solution)/shard_map/jit(_take)/gather | solution.py:71
  99.9 5.9 %reduce.3 = bf16[1024,320]{1,0:T(8,128)(2,1)S(1)} reduce(bf16[1024,1,320]{2,1,0:T(2,128)(2,1)S(1)} %bitcast.93, bf16[]{:T(256)} %broadcast.314), dimensions={1}, to_apply=%bitcast.86.reduce_sub_computation | reduce | bytes 1310722
  106.6 22.7 %all_to_all.37 = bf16[128,2,1280]{2,1,0:T(2,128)(2,1)S(1)} all-to-all(bf16[128,2,1280]{2,1,0:T(2,128)(2,1)S(1)} %reshape.300), channel_id=1, replica_groups=mesh['row'=16,'col'=8] {'row','col'}, dimensions={0} | all-to-all | bytes 1310720 | tf_op jit(solution)/shard_map/all_to_all | solution.py:74
  130.7 1.5 copy.14
  132.2 47.3 %all-gather.7.cloned.1.call-done = bf16[128,1,320,128]{0,2,1,3:T(8,128)(2,1)} async-done(((bf16[128,1,320,8]{0,2,1,3:T(8,128)(2,1)}), bf16[128,1,320,128]{0,2,1,3:T(8,128)(2,1)}) %all-gather.7.cloned.1.call-update) | async-done | bytes 10485776 | tf_op jit(solution)/shard_map/all_gather | solution.py:79
  179.6 15.6 %copy.18 = bf16[128,1,320,128]{3,0,2,1:T(8,128)(2,1)} copy(bf16[128,1,320,128]{0,2,1,3:T(8,128)(2,1)} %all-gather.7.cloned.1.call-done) | data formatting | bytes 20971520 | tf_op jit(solution)/shard_map/all_gather | solution.py:79
  195.2 7.1 %fusion.84 = bf16[128,160,128]{2,0,1:T(8,128)(2,1)} fusion(bf16[128,320,128]{2,0,1:T(8,128)(2,1)} %bitcast.88), kind=kLoop, calls=%fused_computation.34.clone.1 | loop fusion | bytes 10485760 | tf_op jit(solution)/shard_map/wfa,wfb->fab/dot_general | solution.py:39
  202.3 3.4 %fusion.86 = bf16[128,160,128]{2,0,1:T(8,128)(2,1)} fusion(bf16[128,320,128]{2,0,1:T(8,128)(2,1)S(1)} %bitcast.89), kind=kLoop, calls=%fused_computation.32.clone.clone.clone.1 | loop fusion | bytes 10485760 | tf_op jit(solution)/shard_map/wfa,wfb->fab/dot_general | solution.py:39
  205.7 3.5 %fusion.82 = bf16[128,160,128]{2,0,1:T(8,128)(2,1)} fusion(bf16[128,320,128]{2,0,1:T(8,128)(2,1)S(1)} %bitcast.90), kind=kLoop, calls=%fused_computation.33.clone.1 | loop fusion | bytes 10485760 | tf_op jit(solution)/shard_map/wfa,wfb->fab/dot_general | solution.py:39
  209.2 3.4 %fusion.88 = bf16[128,160,128]{2,0,1:T(8,128)(2,1)} fusion(bf16[128,320,128]{2,0,1:T(8,128)(2,1)S(1)} %bitcast.91), kind=kLoop, calls=%fused_computation.35.clone.clone.clone.1 | loop fusion | bytes 10485760 | tf_op jit(solution)/shard_map/wfa,wfb->fab/dot_general | solution.py:39
  212.6 84.4 %all-gather.5.cloned.1.call-done = bf16[128,1,320,64]{0,3,2,1:T(8,128)(2,1)} async-done(((bf16[128,1,320,8]{0,3,2,1:T(8,128)(2,1)}), bf16[128,1,320,64]{0,3,2,1:T(8,128)(2,1)}) %all-gather.5.cloned.1.call-update) | async-done | bytes 5242896 | tf_op jit(solution)/shard_map/all_gather | solution.py:77
  296.9 7.2 %fusion.13 = f32[160,64,128]{2,1,0:T(8,128)} fusion(bf16[128,1,320,64]{0,3,2,1:T(8,128)(2,1)} %all-gather.5.cloned.1.call-done, bf16[128,160,128]{2,0,1:T(8,128)(2,1)} %fusion.84), kind=kOutput, calls=%fused_computation.21 | convolution fusion | flops 335544320 | bytes 15728640 | tf_op jit(solution)/shard_map/wfa,wfb->fab/dot_general | solution.py:39
  304.3 3.8 %fusion.9 = f32[160,64,128]{2,1,0:T(8,128)} fusion(bf16[128,1,320,64]{0,3,2,1:T(8,128)(2,1)S(1)} %copy-done, bf16[128,160,128]{2,0,1:T(8,128)(2,1)S(1)} %copy-done.5), kind=kOutput, calls=%fused_computation.17 | convolution fusion | flops 335544320 | bytes 15728640 | tf_op jit(solution)/shard_map/wfa,wfb->fab/dot_general | solution.py:39
  308.1 4.1 %subtract_bitcast_fusion = f32[1,160,64,128]{3,2,1,0:T(8,128)S(1)} fusion(f32[160,64,128]{2,1,0:T(8,128)} %fusion.13, bf16[128,1,320,64]{0,3,2,1:T(8,128)(2,1)S(1)} %copy-done, bf16[128,160,128]{2,0,1:T(8,128)(2,1)S(1)} %copy-done.4), kind=kOutput, calls=%fused_computation.25 | convolution fusion | flops 336855040 | bytes 20971520 | tf_op jit(solution)/shard_map/wfa,wfb->fab/dot_general | solution.py:39
  312.2 4.0 %add_bitcast_fusion = f32[1,160,64,128]{3,2,1,0:T(8,128)S(1)} fusion(f32[160,64,128]{2,1,0:T(8,128)} %fusion.9, bf16[128,1,320,64]{0,3,2,1:T(8,128)(2,1)S(1)} %copy-done, bf16[128,160,128]{2,0,1:T(8,128)(2,1)S(1)} %copy-done.3), kind=kOutput, calls=%fused_computation.26 | convolution fusion | flops 336855040 | bytes 20971520 | tf_op jit(solution)/shard_map/wfa,wfb->fab/dot_general | solution.py:39
  316.2 3.9 %fusion.4 = bf16[2,160,64,128]{3,2,1,0:T(8,128)(2,1)} fusion(f32[1,160,64,128]{3,2,1,0:T(8,128)S(1)} %subtract_bitcast_fusion, f32[1,160,64,128]{3,2,1,0:T(8,128)S(1)} %add_bitcast_fusion), kind=kLoop, calls=%fused_computation.10 | loop fusion | flops 7864320 | bytes 15728640 | tf_op jit(solution)/shard_map/convert_element_type | solution.py:81
  (46 shorter events, 10.0 us)
Async XLA Ops:
  6.5 173.0 %all-gather.7.cloned.1.call-start = ((), (), s32[]{:S(2)}) async-start(), calls=%async_computation.3 | async-start | bytes 11141120 | tf_op jit(solution)/shard_map/all_gather | solution.py:79
  7.3 7.2 %copy-start.1 = (s32[1024]{0:T(1024)S(1)}, s32[1024]{0:T(1024)}, u32[]{:S(2)}) copy-start(s32[1024]{0:T(1024)} %param.9) | copy-start | bytes 12292
  7.3 11.8 %copy-start.6 = (s32[10]{0:T(128)S(1)}, s32[10]{0:T(128)}, u32[]{:S(2)}) copy-start(s32[10]{0:T(128)} %param.8) | copy-start | bytes 124
  94.2 202.7 %all-gather.5.cloned.1.call-start = ((), (), s32[]{:S(2)}) async-start(), calls=%async_computation.2 | async-start | bytes 5898240 | tf_op jit(solution)/shard_map/all_gather | solution.py:77
  195.2 7.1 %copy-start.2 = (bf16[128,1,320,128]{3,0,2,1:T(8,128)(2,1)S(1)}, bf16[128,1,320,128]{3,0,2,1:T(8,128)(2,1)}, u32[]{:S(2)}) copy-start(bf16[128,1,320,128]{3,0,2,1:T(8,128)(2,1)} %copy.18) | copy-start | bytes 31457284
  296.9 7.2 %copy-start = (bf16[128,1,320,64]{0,3,2,1:T(8,128)(2,1)S(1)}, bf16[128,1,320,64]{0,3,2,1:T(8,128)(2,1)}, u32[]{:S(2)}) copy-start(bf16[128,1,320,64]{0,3,2,1:T(8,128)(2,1)} %all-gather.5.cloned.1.call-done) | copy-start | bytes 15728644
  296.9 7.3 %copy-start.5 = (bf16[128,160,128]{2,0,1:T(8,128)(2,1)S(1)}, bf16[128,160,128]{2,0,1:T(8,128)(2,1)}, u32[]{:S(2)}) copy-start(bf16[128,160,128]{2,0,1:T(8,128)(2,1)} %fusion.82) | copy-start | bytes 15728644
  304.3 3.8 %copy-start.4 = (bf16[128,160,128]{2,0,1:T(8,128)(2,1)S(1)}, bf16[128,160,128]{2,0,1:T(8,128)(2,1)}, u32[]{:S(2)}) copy-start(bf16[128,160,128]{2,0,1:T(8,128)(2,1)} %fusion.86) | copy-start | bytes 15728644
  308.1 4.1 %copy-start.3 = (bf16[128,160,128]{2,0,1:T(8,128)(2,1)S(1)}, bf16[128,160,128]{2,0,1:T(8,128)(2,1)}, u32[]{:S(2)}) copy-start(bf16[128,160,128]{2,0,1:T(8,128)(2,1)} %fusion.88) | copy-start | bytes 15728644
Sparse Core Ops, SparseCore 0:
  94.3 85.1 all-gather.6
  181.1 115.7 all-gather.4
where the time goes:
time: 333 us; the launch traced here: 327 us
  waiting for transfers between devices  132 us (40%)
  local copies, waits for them, and re-layouts  56.6 us (17%)
  other arithmetic  48.2 us (14%)
  blocking collectives  45.3 us (14%)
  matrix products  31.3 us (9%)
  between operations  14.1 us (4%)
    all_gather x1, waiting for transfers between devices, body(): row_block = lax.all_gather(row_local, 'col', axis=2, tiled=True)  84.4 us
    all_gather x1, waiting for transfers between devices, body(): col_block = lax.all_gather(col_local, 'row', axis=2, tiled=True)  47.3 us
    cos x1, other arithmetic, make_table(): jnp.cos(angles)  23.5 us
    all_to_all x1, blocking collectives, body(): lax.all_to_all(row_source, ('row', 'col'), split_axis=2, concat_axis=0, t...  22.7 us
    all_to_all x1, blocking collectives, body(): lax.all_to_all(col_source, ('row', 'col'), split_axis=2, concat_axis=0, t...  22.6 us
    dot_general x4, matrix products, pair_product(): jnp.einsum('wfa,wfb->fab', left, right, preferred_element_type=jnp.float32)  19.1 us
    dot_general x4, local copies, waits for them, and re-layouts, pair_product(): jnp.einsum('wfa,wfb->fab', left, right, preferred_element_type=jnp.float32)  17.4 us
    all_gather x1, local copies, waits for them, and re-layouts, body(): col_block = lax.all_gather(col_local, 'row', axis=2, tiled=True)  15.6 us
  transfers between devices with their start and end apart: 2, of which 2 were waited for; matrix products, arithmetic and copies ran while one was open for 15% of the time, Pallas kernels for 0%

commit v1 on v0

v1 whole, which is shorter than its diff:
```python
import functools
import itertools
import math

import jax
import jax.numpy as jnp
from jax import lax
from jax.experimental import pallas as pl
from jax.experimental.pallas import tpu as pltpu
from jax.sharding import PartitionSpec as P

BINS = 16
AXES = ("row", "col")
SIZES = (4, 2, 2, 4, 2)
GROUPS = 8
CHUNKS = (8, 12)
VMEM = 56 * 1024 * 1024


def coordinates():
    row = lax.axis_index("row")
    col = lax.axis_index("col")
    x, z_hi, core = row // 4, row // 2 % 2, row % 2
    y, z_lo = col // 2, col % 2
    return x, y, z_hi * 2 + z_lo, core


def permute(array, move):
    pairs = []
    for source, (x, z_hi, core, y, z_lo) in enumerate(
        itertools.product(*(range(size) for size in SIZES))
    ):
        x2, y2, z2, core2 = move(x, y, z_hi * 2 + z_lo, core)
        target = (((x2 % 4 * 2 + z2 % 4 // 2) * 2 + core2 % 2) * 4 + y2 % 4) * 2 + z2 % 2
        pairs.append((source, target))
    return lax.ppermute(array, AXES, pairs)


def split_dot(left, right, dims):
    total = None
    for _ in range(3):
        term = right.astype(jnp.bfloat16)
        right = right - term.astype(jnp.float32)
        part = lax.dot_general(left, term, dims, preferred_element_type=jnp.float32)
        total = part if total is None else total + part
    return total


def spectra_kernel(
    place_ref, band_ref, wave_ref, mask_ref, map_ref, *refs, length, band_count, chunks
):
    outs = refs[: len(chunks) * GROUPS]
    table_ref, white_ref = refs[len(chunks) * GROUPS :]
    step = pl.program_id(0)
    bins = band_count * BINS
    width = wave_ref.shape[0]
    stations = white_ref.shape[1]
    lanes = 128

    @pl.when(step == 0)
    def _():
        band = lax.broadcasted_iota(jnp.int32, (bins, lanes), 0) // BINS
        lane = lax.broadcasted_iota(jnp.int32, (bins, lanes), 1)
        frequency = lax.broadcasted_iota(jnp.int32, (bins, lanes), 0) % BINS
        for b in range(band_count):
            frequency = frequency + jnp.where(band == b, band_ref[b], 0)
        unit = jnp.float32(2.0 * math.pi / length)
        scaling = jnp.float32(length ** (-0.5))
        fine = (frequency * lane % length).astype(jnp.float32) * unit
        coarse = (frequency * (lane * lanes % length) % length).astype(jnp.float32) * unit
        fine_cos = jnp.cos(fine) * scaling
        fine_sin = jnp.sin(fine) * scaling
        coarse_cos = jnp.cos(coarse)
        coarse_sin = jnp.sin(coarse)
        for part in range(length // lanes):
            c = coarse_cos[:, part : part + 1]
            s = coarse_sin[:, part : part + 1]
            columns = slice(part * lanes, (part + 1) * lanes)
            table_ref[:bins, columns] = (c * fine_cos - s * fine_sin).astype(jnp.bfloat16)
            table_ref[bins:, columns] = (-s * fine_cos - c * fine_sin).astype(jnp.bfloat16)

    spectra = lax.dot_general(
        table_ref[...], wave_ref[...], (((1,), (1,)), ((), ())), preferred_element_type=jnp.float32
    )
    squares = jnp.zeros((width, lanes), jnp.float32)
    for part in range(length // lanes):
        piece = wave_ref[:, part * lanes : (part + 1) * lanes].astype(jnp.float32)
        squares = squares + piece * piece
    ones = jnp.ones((8, lanes), jnp.bfloat16)
    total = split_dot(ones, squares, (((1,), (1,)), ((), ())))[:1]
    inverse = lax.rsqrt(total / length + 1e-06)
    real_part = spectra[:bins] * inverse
    imag_part = spectra[bins:] * inverse
    power = real_part * real_part + imag_part * imag_part
    banded = power.reshape(band_count, BINS, width)
    mean = jnp.broadcast_to(jnp.mean(banded, axis=1, keepdims=True), banded.shape)
    mask = mask_ref[...].astype(jnp.float32)
    factor = mask * lax.rsqrt(power + mean.reshape(bins, width) + 0.1)
    columns = pl.ds(pl.multiple_of(step * width, width), width)
    white_ref[:bins, columns] = (real_part * factor).astype(jnp.bfloat16)
    white_ref[bins:, columns] = (imag_part * factor).astype(jnp.bfloat16)

    @pl.when(step == pl.num_programs(0) - 1)
    def _():
        z, core = place_ref[2], place_ref[3]
        rows = 2 * bins
        goal = lax.broadcasted_iota(jnp.int32, (rows, 1), 0)
        source = jnp.zeros((rows, 1), jnp.int32)
        start = 0
        for nb in chunks:
            base = 2 * GROUPS * start
            local = goal - base
            slot = local // (2 * nb)
            within = local % (2 * nb)
            group = (z + slot // 2) % 4 * 2 + (core + slot) % 2
            picked = within // nb * bins + GROUPS * start + group * nb + within % nb
            inside = (local >= 0) & (local < 2 * GROUPS * nb)
            source = jnp.where(inside, picked, source)
            start += nb
        order = lax.broadcasted_iota(jnp.int32, (rows, rows), 1) == source
        order = order.astype(jnp.float32).astype(jnp.bfloat16)
        sorted_rows = jnp.dot(
            order, white_ref[...], preferred_element_type=jnp.float32
        ).astype(jnp.bfloat16)
        block = 256
        for first in range(0, stations, block):
            station = lax.broadcasted_iota(jnp.int32, (stations, block), 0)
            take = station == map_ref[:, first : first + block]
            take = take.astype(jnp.float32).astype(jnp.bfloat16)
            moved = jnp.dot(sorted_rows, take, preferred_element_type=jnp.float32)
            moved = moved.astype(jnp.bfloat16)
            row = 0
            for c, nb in enumerate(chunks):
                for slot in range(GROUPS):
                    outs[c * GROUPS + slot][:, first : first + block] = moved[row : row + 2 * nb]
                    row += 2 * nb


def make_spectra(place, waveform, valid_mask, band_starts, station_map, chunks):
    stations, length = waveform.shape
    band_count = band_starts.shape[0]
    rows = 2 * BINS * band_count
    width = 256
    shapes = [
        jax.ShapeDtypeStruct((2 * nb, stations), jnp.bfloat16) for nb in chunks for _ in range(GROUPS)
    ]
    smem = pl.BlockSpec(memory_space=pltpu.SMEM)
    return pl.pallas_call(
        functools.partial(spectra_kernel, length=length, band_count=band_count, chunks=chunks),
        grid=(stations // width,),
        in_specs=[
            smem,
            smem,
            pl.BlockSpec((width, length), lambda i: (i, 0)),
            pl.BlockSpec((1, width), lambda i: (0, i)),
            pl.BlockSpec((1, stations), lambda i: (0, 0)),
        ],
        out_specs=[pl.BlockSpec(s.shape, lambda i: (0, 0)) for s in shapes],
        out_shape=shapes,
        scratch_shapes=[
            pltpu.VMEM((rows, length), jnp.bfloat16),
            pltpu.VMEM((rows, stations), jnp.bfloat16),
        ],
        compiler_params=pltpu.CompilerParams(vmem_limit_bytes=VMEM),
        cost_estimate=pl.CostEstimate(
            flops=2 * rows * length * stations, bytes_accessed=2 * stations * length, transcendentals=0
        ),
        name="spectra",
    )(place, band_starts, waveform, valid_mask, station_map)


def weave_kernel(place_ref, *refs, nb):
    ins, outs, woven_ref = refs[:GROUPS], refs[GROUPS:-1], refs[-1]
    x, y = place_ref[0], place_ref[1]
    stacked = jnp.stack([ref[...].astype(jnp.float32) for ref in ins], axis=0)
    stacked = jnp.swapaxes(stacked, 0, 1)
    woven_ref[...] = jnp.concatenate([stacked[:nb], stacked[nb:]], axis=1).astype(jnp.bfloat16)
    block = outs[0].shape[2]
    for side, own in enumerate((x, y)):
        for k in range(4):
            first = pl.multiple_of((own + k) % 4 * block, block)
            outs[side * 4 + k][...] = woven_ref[:, :, pl.ds(first, block)]


def weave(place, slots, nb):
    stations = slots[0].shape[1]
    shape = jax.ShapeDtypeStruct((nb, 16, stations // 4), jnp.bfloat16)
    return pl.pallas_call(
        functools.partial(weave_kernel, nb=nb),
        in_specs=[pl.BlockSpec(memory_space=pltpu.SMEM)]
        + [pl.BlockSpec(memory_space=pltpu.VMEM)] * GROUPS,
        out_specs=[pl.BlockSpec(memory_space=pltpu.VMEM)] * 8,
        out_shape=[shape] * 8,
        scratch_shapes=[pltpu.VMEM((nb, 16, stations), jnp.bfloat16)],
        compiler_params=pltpu.CompilerParams(vmem_limit_bytes=VMEM),
        name="weave",
    )(place, *slots)


def product_kernel(place_ref, *refs, scaling):
    rows, cols, outs, scratch = refs[:4], refs[4:8], refs[8:16], refs[16]
    z, core = place_ref[2], place_ref[3]
    count = rows[0].shape[1]
    for j in range(count):
        left = jnp.concatenate([rows[ky][kx, j] for kx in range(4) for ky in range(4)], axis=0)
        pieces = [cols[kx][ky, j] for kx in range(4) for ky in range(4)]
        right = jnp.concatenate(pieces, axis=0)
        wide = right.astype(jnp.float32).reshape(16, 2, 8, right.shape[1])
        turned = jnp.concatenate([wide[:, 1:], -wide[:, :1]], axis=1)
        turned = turned.reshape(right.shape).astype(jnp.bfloat16)
        dims = (((0,), (0,)), ((), ()))
        for part, operand in enumerate((right, turned)):
            result = lax.dot_general(left, operand, dims, preferred_element_type=jnp.float32)
            scratch[part, j] = (result * scaling).astype(jnp.bfloat16)
    for slot in range(GROUPS):
        goal_z = (z + slot // 2) % 4
        first_row = pl.multiple_of(goal_z // 2 * 128 + (core + slot) % 2 * 64, 64)
        first_col = pl.multiple_of(goal_z % 2 * 128, 128)
        outs[slot][...] = scratch[:, :, pl.ds(first_row, 64), pl.ds(first_col, 128)]


def product(place, rows, cols, nb, scaling):
    per_step = 4
    block = rows[0].shape[-1]
    shape = jax.ShapeDtypeStruct((2, nb, 64, 128), jnp.bfloat16)
    spec = pl.BlockSpec((4, per_step, 16, block), lambda i: (0, i, 0, 0))
    return pl.pallas_call(
        functools.partial(product_kernel, scaling=scaling),
        grid=(nb // per_step,),
        in_specs=[pl.BlockSpec(memory_space=pltpu.SMEM)] + [spec] * 8,
        out_specs=[pl.BlockSpec((2, per_step, 64, 128), lambda i: (0, i, 0, 0))] * GROUPS,
        out_shape=[shape] * GROUPS,
        scratch_shapes=[pltpu.VMEM((2, per_step, block, block), jnp.bfloat16)],
        compiler_params=pltpu.CompilerParams(vmem_limit_bytes=VMEM),
        cost_estimate=pl.CostEstimate(
            flops=4 * nb * block**3, bytes_accessed=8 * nb * block * block * 2, transcendentals=0
        ),
        name="product",
    )(place, *rows, *cols)


def place_kernel(place_ref, *refs, start, nb, aliased):
    ins = refs[:GROUPS]
    out, sems = refs[GROUPS + aliased], refs[-1]
    z, core = place_ref[2], place_ref[3]
    copies = []
    for slot in range(GROUPS):
        group = (z + 4 - slot // 2) % 4 * 2 + (core + slot) % 2
        first = group * sum(CHUNKS) + start
        copies.append(pltpu.make_async_copy(ins[slot], out.at[:, pl.ds(first, nb)], sems.at[slot]))
    for copy in copies:
        copy.start()
    for copy in copies:
        copy.wait()


def place_blocks(place, slots, total, start, nb, shape):
    aliased = total is not None
    anywhere = pl.BlockSpec(memory_space=pl.ANY)
    operands = [place, *slots] + ([total] if aliased else [])
    return pl.pallas_call(
        functools.partial(place_kernel, start=start, nb=nb, aliased=aliased),
        in_specs=[pl.BlockSpec(memory_space=pltpu.SMEM)]
        + [pl.BlockSpec(memory_space=pltpu.VMEM)] * GROUPS
        + [anywhere] * aliased,
        out_specs=anywhere,
        out_shape=shape,
        scratch_shapes=[pltpu.SemaphoreType.DMA((GROUPS,))],
        input_output_aliases={len(operands) - 1: 0} if aliased else {},
        compiler_params=pltpu.CompilerParams(vmem_limit_bytes=VMEM),
        name="place",
    )(*operands)


def exchange(slots):
    return [slots[0]] + [
        permute(
            slots[slot],
            lambda x, y, z, core, slot=slot: (x, y, z + slot // 2, core + slot),
        )
        for slot in range(1, GROUPS)
    ]


def along(array, axis, k):
    if axis == "x":
        return permute(array, lambda x, y, z, core: (x + k, y, z, core))
    return permute(array, lambda x, y, z, core: (x, y + k, z, core))


def body(waveform, valid_mask, band_starts, station_map):
    place = jnp.stack(coordinates()).astype(jnp.int32)
    stations = waveform.shape[1]
    windows = waveform.shape[0] * lax.axis_size("row") * lax.axis_size("col")
    bins = BINS * band_starts.shape[0]
    scaling = float(windows) ** (-0.5)
    spectra = make_spectra(
        place, waveform[0], valid_mask, band_starts, station_map.reshape(1, stations), (bins // GROUPS,)
    )
    shape = jax.ShapeDtypeStruct((2, bins, 64, 128), jnp.bfloat16)
    woven = weave(place, exchange(spectra), bins // GROUPS)
    row_parts = [woven[0]] + [along(woven[k], "x", k) for k in (1, 2, 3)]
    col_parts = [woven[4]] + [along(woven[4 + k], "y", k) for k in (1, 2, 3)]
    total = None
    start = 0
    for nb in CHUNKS:
        row_shard = jnp.stack([part[start : start + nb] for part in row_parts], axis=0)
        col_shard = jnp.stack([part[start : start + nb] for part in col_parts], axis=0)
        rows = [row_shard] + [along(row_shard, "y", k) for k in (1, 2, 3)]
        cols = [col_shard] + [along(col_shard, "x", k) for k in (1, 2, 3)]
        blocks = exchange(product(place, rows, cols, nb, scaling))
        total = place_blocks(place, blocks, total, start, nb, shape)
        start += nb
    return total


def solution(mesh):
    placed = (P(AXES, None, None), P(AXES, None), P(), P())
    return jax.shard_map(
        body, mesh=mesh, in_specs=placed, out_specs=P(None, None, "row", "col"), check_vma=False
    )
```

time: 333 us -> 175 us (0.53); the launches traced: 327 us -> 174 us
  waiting for transfers between devices: 132 us -> 69.4 us
  starting transfers between devices: 0.04 us -> 60 us
  local copies, waits for them, and re-layouts: 56.6 us -> 5.74 us
  other arithmetic: 48.2 us -> 0.83 us
  blocking collectives: 45.3 us -> 0 us
  Pallas kernels: 0 us -> 37.5 us
  matrix products: 31.3 us -> 0 us
  between operations: 14.1 us -> 0.65 us
    all_gather x2 -> x0, waiting for transfers between devices: 132 us -> none  [the longest x1 84.4 us: body(): row_block = lax.all_gather(row_local, 'col', axis=2, tiled=True)]
    ppermute x0 -> x39, waiting for transfers between devices: none -> 69.4 us  [permute(): return lax.ppermute(array, AXES, pairs)]
    ppermute x0 -> x39, starting transfers between devices: none -> 60 us  [permute(): return lax.ppermute(array, AXES, pairs)]
    all_to_all x2 -> x0, blocking collectives: 45.3 us -> none  [the longest x1 22.7 us: body(): lax.all_to_all(row_source, ('row', 'col'), split_axis=2, concat_axis=0, t...]
    pallas_call x0 -> x6, Pallas kernels: none -> 37.5 us  [the longest x1 19.3 us: make_spectra(): pl.pallas_call(functools.partial(spectra_kernel, length=length, band_coun...]
    dot_general x5 -> x0, matrix products: 31.3 us -> none  [the longest x4 19.1 us: pair_product(): jnp.einsum('wfa,wfb->fab', left, right, preferred_element_type=jnp.float32)]
    cos x1 -> x0, other arithmetic: 23.5 us -> none  [make_table(): jnp.cos(angles)]
    dot_general x4 -> x0, local copies, waits for them, and re-layouts: 17.4 us -> none  [pair_product(): jnp.einsum('wfa,wfb->fab', left, right, preferred_element_type=jnp.float32)]
  transfers between devices with their start and end apart: 2 -> 39, of which waited for: 2 -> 15; matrix products, arithmetic and copies ran while one was open for 15% -> 1% of each run, Pallas kernels for 0% -> 7%
where the time goes in v1:
time: 175 us; the launch traced here: 174 us
  waiting for transfers between devices  69.4 us (40%)
  starting transfers between devices  60 us (34%)
  Pallas kernels  37.5 us (21%)
  local copies, waits for them, and re-layouts  5.74 us (3%)
    ppermute x39, waiting for transfers between devices, permute(): return lax.ppermute(array, AXES, pairs)  69.4 us
    ppermute x39, starting transfers between devices, permute(): return lax.ppermute(array, AXES, pairs)  60 us
    pallas_call x1, Pallas kernels, make_spectra(): pl.pallas_call(functools.partial(spectra_kernel, length=length, band_coun...  19.3 us
    pallas_call x2, Pallas kernels, product(): pl.pallas_call(functools.partial(product_kernel, scaling=scaling), grid=(...  9.08 us
    pallas_call x2, Pallas kernels, place_blocks(): pl.pallas_call(functools.partial(place_kernel, start=start, nb=nb, aliase...  6.54 us
  transfers between devices with their start and end apart: 39, of which 15 were waited for; matrix products, arithmetic and copies ran while one was open for 1% of the time, Pallas kernels for 7%

profile of v1, /device:TPU:15, one launch (start us, length us, event | category | flops | bytes accessed | tf_op | source)
XLA Modules:
  0.0 174.1 jit_solution(9382803357571366689)
XLA Ops:
  0.7 19.3 %spectra.1 = (bf16[40,1024]{1,0:T(8,128)(2,1)}, bf16[40,1024]{1,0:T(8,128)(2,1)}, bf16[40,1024]{1,0:T(8,128)(2,1)}, bf16[40,1024]{1,0:T(8,128)(2,1)}, bf16[40,10...) custom-call(s32[4]{0:T(128)} %pad_add_fusion.place_ref, ...), custom_call_target="tpu_custom_call" | custom-call | flops 5368709120 | bytes 16777216 | tf_op jit(solution)/shard_map/spectra/pallas_call | solution.py:148
  29.8 2.0 %collective-permute-done.3.refs_4_ = bf16[40,1024]{1,0:T(8,128)(2,1)S(1)} collective-permute-done((bf16[40,1024]{1,0:T(8,128)(2,1)}, bf16[40,1024]{1,0:T(8,128)(2,1)S(1)}, u32[]{:S(2)}, u32[]{:S(2)}) %collective-permute-start.3) | collective-permute-done | bytes 81952 | tf_op jit(solution)/shard_map/ppermute | solution.py:36
  35.9 2.6 %weave.1 = (bf16[20,16,256]{2,1,0:T(8,128)(2,1)}, bf16[20,16,256]{2,1,0:T(8,128)(2,1)}, bf16[20,16,256]{2,1,0:T(8,128)(2,1)}, bf16[20,16,256]{2,1,0:T(8,128)(2,1...) custom-call(s32[4]{0:T(128)} %pad_add_fusion.place_ref, ...), custom_call_target="tpu_custom_call" | custom-call | tf_op jit(solution)/shard_map/weave/pallas_call | solution.py:188
  41.4 2.1 %collective-permute-start.8 = (bf16[20,16,256]{2,1,0:T(8,128)(2,1)}, bf16[20,16,256]{2,1,0:T(8,128)(2,1)S(1)}, u32[]{:S(2)}, u32[]{:S(2)}) collective-permute-start(bf16[20,16,256]{2,1,0:T(8,128)(2,1)} %get-tuple-element.47), channel_id=1, source_target_pairs={{0,64},{1,65},{2,66},{3,67},{4,68},{5,69},{6,70},{7,71},{8,72},{9,... | collective-permute-start | bytes 491528 | tf_op jit(solution)/shard_map/ppermute | solution.py:36
  46.4 2.1 %collective-permute-done.13 = bf16[20,16,256]{2,1,0:T(8,128)(2,1)S(1)} collective-permute-done((bf16[20,16,256]{2,1,0:T(8,128)(2,1)}, bf16[20,16,256]{2,1,0:T(8,128)(2,1)S(1)}, u32[]{:S(2)}, u32[]{:S(2)}) %collective-permute-start.13) | collective-permute-done | bytes 163872 | tf_op jit(solution)/shard_map/ppermute | solution.py:36
  51.0 3.2 %collective-permute-done.15 = bf16[20,16,256]{2,1,0:T(8,128)(2,1)S(1)} collective-permute-done((bf16[20,16,256]{2,1,0:T(8,128)(2,1)}, bf16[20,16,256]{2,1,0:T(8,128)(2,1)S(1)}, u32[]{:S(2)}, u32[]{:S(2)}) %collective-permute-start.15) | collective-permute-done | bytes 163872 | tf_op jit(solution)/shard_map/ppermute | solution.py:36
  55.1 3.3 %collective-permute-start.30 = (bf16[4,8,16,256]{3,2,1,0:T(8,128)(2,1)S(1)}, bf16[4,8,16,256]{3,2,1,0:T(8,128)(2,1)S(1)}, u32[]{:S(2)}, u32[]{:S(2)}) collective-permute-start(bf16[4,8,16,256]{3,2,1,0:T(8,128)(2,1)S(1)} %pad_maximum_fusion.3.refs_4_), channel_id=1, source_target_pairs={{0,64},{1,65},{2,66},{3,67},{4,68},{5,69},{6,70},{7,71},{8,72},{9,... | collective-permute-start | bytes 786440 | tf_op jit(solution)/shard_map/ppermute | solution.py:36
  63.2 2.2 %collective-permute-done.30.refs_6_ = bf16[4,8,16,256]{3,2,1,0:T(8,128)(2,1)S(1)} collective-permute-done((bf16[4,8,16,256]{3,2,1,0:T(8,128)(2,1)S(1)}, bf16[4,8,16,256]{3,2,1,0:T(8,128)(2,1)S(1)}, u32[]{:S(2)}, u32[]{:S(2)}) %collective-permute-start.30) | collective-permute-done | bytes 262176 | tf_op jit(solution)/shard_map/ppermute | solution.py:36
  65.4 2.2 %collective-permute-start.17 = (bf16[4,12,16,256]{3,2,1,0:T(8,128)(2,1)S(1)}, bf16[4,12,16,256]{3,2,1,0:T(8,128)(2,1)S(1)}, u32[]{:S(2)}, u32[]{:S(2)}) collective-permute-start(bf16[4,12,16,256]{3,2,1,0:T(8,128)(2,1)S(1)} %pad_maximum_fusion.1.refs_4_), channel_id=1, source_target_pairs={{0,64},{1,65},{2,66},{3,67},{4,68},{5,69},{6,70},{7,71},{8,72},{9,... | collective-permute-start | bytes 1179656 | tf_op jit(solution)/shard_map/ppermute | solution.py:36
  68.7 4.1 %collective-permute-start.12 = (bf16[4,12,16,256]{3,2,1,0:T(8,128)(2,1)S(1)}, bf16[4,12,16,256]{3,2,1,0:T(8,128)(2,1)S(1)}, u32[]{:S(2)}, u32[]{:S(2)}) collective-permute-start(bf16[4,12,16,256]{3,2,1,0:T(8,128)(2,1)S(1)} %pad_maximum_fusion.refs_0_), channel_id=1, source_target_pairs={{0,6},{1,7},{2,0},{3,1},{4,2},{5,3},{6,4},{7,5},{8,14},{9,15},{10,... | collective-permute-start | bytes 1179656 | tf_op jit(solution)/shard_map/ppermute | solution.py:36
  72.8 4.3 %collective-permute-done.18.refs_7_ = bf16[4,12,16,256]{3,2,1,0:T(8,128)(2,1)S(1)} collective-permute-done((bf16[4,12,16,256]{3,2,1,0:T(8,128)(2,1)S(1)}, bf16[4,12,16,256]{3,2,1,0:T(8,128)(2,1)S(1)}, u32[]{:S(2)}, u32[]{:S(2)}) %collective-permute-start.18) | collective-permute-done | bytes 393248 | tf_op jit(solution)/shard_map/ppermute | solution.py:36
  77.1 3.8 %product.3 = (bf16[2,8,64,128]{3,2,1,0:T(8,128)(2,1)}, bf16[2,8,64,128]{3,2,1,0:T(8,128)(2,1)}, bf16[2,8,64,128]{3,2,1,0:T(8,128)(2,1)}, bf16[2,8,64,128]{3,2,1,...) custom-call(s32[4]{0:T(128)} %pad_add_fusion.place_ref, ...), custom_call_target="tpu_custom_call" | custom-call | flops 536870912 | bytes 8388608 | tf_op jit(solution)/shard_map/product/pallas_call | solution.py:227
  82.8 12.8 %collective-permute-start.32 = (bf16[2,8,64,128]{3,2,1,0:T(8,128)(2,1)}, bf16[2,8,64,128]{3,2,1,0:T(8,128)(2,1)S(1)}, u32[]{:S(2)}, u32[]{:S(2)}) collective-permute-start(bf16[2,8,64,128]{3,2,1,0:T(8,128)(2,1)} %get-tuple-element.62), channel_id=1, source_target_pairs={{0,8},{1,9},{2,10},{3,11},{4,12},{5,13},{6,14},{7,15},{8,0},{9,1},... | collective-permute-start | bytes 786440 | tf_op jit(solution)/shard_map/ppermute | solution.py:36
  97.4 2.4 %collective-permute-start.35 = (bf16[2,8,64,128]{3,2,1,0:T(8,128)(2,1)}, bf16[2,8,64,128]{3,2,1,0:T(8,128)(2,1)S(1)}, u32[]{:S(2)}, u32[]{:S(2)}) collective-permute-start(bf16[2,8,64,128]{3,2,1,0:T(8,128)(2,1)} %get-tuple-element.65), channel_id=1, source_target_pairs={{0,16},{1,17},{2,18},{3,19},{4,20},{5,21},{6,22},{7,23},{8,24},{9,... | collective-permute-start | bytes 786440 | tf_op jit(solution)/shard_map/ppermute | solution.py:36
  100.5 5.3 %product.2 = (bf16[2,12,64,128]{3,2,1,0:T(8,128)(2,1)}, bf16[2,12,64,128]{3,2,1,0:T(8,128)(2,1)}, bf16[2,12,64,128]{3,2,1,0:T(8,128)(2,1)}, bf16[2,12,64,128]{3,...) custom-call(s32[4]{0:T(128)} %pad_add_fusion.place_ref, ...), custom_call_target="tpu_custom_call" | custom-call | flops 805306368 | bytes 12582912 | tf_op jit(solution)/shard_map/product/pallas_call | solution.py:227
  107.4 2.3 %collective-permute-start.36 = (bf16[2,8,64,128]{3,2,1,0:T(8,128)(2,1)}, bf16[2,8,64,128]{3,2,1,0:T(8,128)(2,1)S(1)}, u32[]{:S(2)}, u32[]{:S(2)}) collective-permute-start(bf16[2,8,64,128]{3,2,1,0:T(8,128)(2,1)} %get-tuple-element.66), channel_id=1, source_target_pairs={{0,24},{1,25},{2,26},{3,27},{4,28},{5,29},{6,30},{7,31},{8,16},{9,... | collective-permute-start | bytes 786440 | tf_op jit(solution)/shard_map/ppermute | solution.py:36
  112.4 4.7 %collective-permute-done.35.refs_4_ = bf16[2,8,64,128]{3,2,1,0:T(8,128)(2,1)S(1)} collective-permute-done((bf16[2,8,64,128]{3,2,1,0:T(8,128)(2,1)}, bf16[2,8,64,128]{3,2,1,0:T(8,128)(2,1)S(1)}, u32[]{:S(2)}, u32[]{:S(2)}) %collective-permute-start.35) | collective-permute-done | bytes 262176 | tf_op jit(solution)/shard_map/ppermute | solution.py:36
  117.1 14.2 %collective-permute-done.36.refs_5_ = bf16[2,8,64,128]{3,2,1,0:T(8,128)(2,1)S(1)} collective-permute-done((bf16[2,8,64,128]{3,2,1,0:T(8,128)(2,1)}, bf16[2,8,64,128]{3,2,1,0:T(8,128)(2,1)S(1)}, u32[]{:S(2)}, u32[]{:S(2)}) %collective-permute-start.36) | collective-permute-done | bytes 262176 | tf_op jit(solution)/shard_map/ppermute | solution.py:36
  132.4 2.4 %collective-permute-start.23 = (bf16[2,12,64,128]{3,2,1,0:T(8,128)(2,1)}, bf16[2,12,64,128]{3,2,1,0:T(8,128)(2,1)S(1)}, u32[]{:S(2)}, u32[]{:S(2)}) collective-permute-start(bf16[2,12,64,128]{3,2,1,0:T(8,128)(2,1)} %get-tuple-element.58), channel_id=1, source_target_pairs={{0,24},{1,25},{2,26},{3,27},{4,28},{5,29},{6,30},{7,31},{8,16},{9,... | collective-permute-start | bytes 1179656 | tf_op jit(solution)/shard_map/ppermute | solution.py:36
  134.8 2.8 %collective-permute-start.24 = (bf16[2,12,64,128]{3,2,1,0:T(8,128)(2,1)}, bf16[2,12,64,128]{3,2,1,0:T(8,128)(2,1)S(1)}, u32[]{:S(2)}, u32[]{:S(2)}) collective-permute-start(bf16[2,12,64,128]{3,2,1,0:T(8,128)(2,1)} %get-tuple-element.59), channel_id=1, source_target_pairs={{0,17},{1,0},{2,19},{3,2},{4,21},{5,4},{6,23},{7,6},{8,25},{9,8},{... | collective-permute-start | bytes 1179656 | tf_op jit(solution)/shard_map/ppermute | solution.py:36
  137.7 3.0 %place.2.refs_8_ = bf16[2,160,64,128]{3,2,1,0:T(8,128)(2,1)} custom-call(s32[4]{0:T(128)} %pad_add_fusion.place_ref, bf16[2,8,64,128]{3,2,1,0:T(8,128)(2,1)} %get-tuple-element.61.refs_0_, bf16[2,8,64,128]{3,2,1,0:T(8,128)(2,1)} %copy-done.23, bf16[2,8,64,128]{3,2,1,0:T(8,128)(2,1)} %copy-done.24, bf16[2,8,64,128]{3,2,1,0:T(8,128)(2,1)} %copy-done.25, ...), custom_call_target="tpu_custom_call" | custom-call | tf_op jit(solution)/shard_map/place/pallas_call | solution.py:261
  140.6 19.9 %collective-permute-done.21.refs_3_ = bf16[2,12,64,128]{3,2,1,0:T(8,128)(2,1)S(1)} collective-permute-done((bf16[2,12,64,128]{3,2,1,0:T(8,128)(2,1)}, bf16[2,12,64,128]{3,2,1,0:T(8,128)(2,1)S(1)}, u32[]{:S(2)}, u32[]{:S(2)}) %collective-permute-start.21) | collective-permute-done | bytes 393248 | tf_op jit(solution)/shard_map/ppermute | solution.py:36
  160.8 8.9 %collective-permute-done.25.refs_7_ = bf16[2,12,64,128]{3,2,1,0:T(8,128)(2,1)S(1)} collective-permute-done((bf16[2,12,64,128]{3,2,1,0:T(8,128)(2,1)}, bf16[2,12,64,128]{3,2,1,0:T(8,128)(2,1)S(1)}, u32[]{:S(2)}, u32[]{:S(2)}) %collective-permute-start.25) | collective-permute-done | bytes 393248 | tf_op jit(solution)/shard_map/ppermute | solution.py:36
  170.4 3.6 %place.3 = bf16[2,160,64,128]{3,2,1,0:T(8,128)(2,1)} custom-call(s32[4]{0:T(128)} %pad_add_fusion.place_ref, bf16[2,12,64,128]{3,2,1,0:T(8,128)(2,1)} %get-tuple-element.53.refs_0_, bf16[2,12,64,128]{3,2,1,0:T(8,128)(2,1)} %copy-done.10, bf16[2,12,64,128]{3,2,1,0:T(8,128)(2,1)} %copy-done.11, ...), custom_call_target="tpu_custom_call", output_to_operand_aliasing={{}: (9, {})} | custom-call | tf_op jit(solution)/shard_map/place/pallas_call | solution.py:261
  (155 shorter events, 40.2 us)
Async XLA Ops:
  41.2 17.1 %collective-permute-start.7 = (bf16[20,16,256]{2,1,0:T(8,128)(2,1)}, bf16[20,16,256]{2,1,0:T(8,128)(2,1)S(1)}, u32[]{:S(2)}, u32[]{:S(2)}) collective-permute-start(bf16[20,16,256]{2,1,0:T(8,128)(2,1)} %get-tuple-element.46), channel_id=1, source_target_pairs={{0,32},{1,33},{2,34},{3,35},{4,36},{5,37},{6,38},{7,39},{8,40},{9,... | collective-permute-start | bytes 491528 | tf_op jit(solution)/shard_map/ppermute | solution.py:36
  41.4 17.9 %collective-permute-start.8 = (bf16[20,16,256]{2,1,0:T(8,128)(2,1)}, bf16[20,16,256]{2,1,0:T(8,128)(2,1)S(1)}, u32[]{:S(2)}, u32[]{:S(2)}) collective-permute-start(bf16[20,16,256]{2,1,0:T(8,128)(2,1)} %get-tuple-element.47), channel_id=1, source_target_pairs={{0,64},{1,65},{2,66},{3,67},{4,68},{5,69},{6,70},{7,71},{8,72},{9,... | collective-permute-start | bytes 491528 | tf_op jit(solution)/shard_map/ppermute | solution.py:36
  43.5 15.7 %collective-permute-start.9 = (bf16[20,16,256]{2,1,0:T(8,128)(2,1)}, bf16[20,16,256]{2,1,0:T(8,128)(2,1)S(1)}, u32[]{:S(2)}, u32[]{:S(2)}) collective-permute-start(bf16[20,16,256]{2,1,0:T(8,128)(2,1)} %get-tuple-element.48), channel_id=1, source_target_pairs={{0,96},{1,97},{2,98},{3,99},{4,100},{5,101},{6,102},{7,103},{8,104... | collective-permute-start | bytes 491528 | tf_op jit(solution)/shard_map/ppermute | solution.py:36
  61.2 11.6 %collective-permute-start.26 = (bf16[4,8,16,256]{3,2,1,0:T(8,128)(2,1)S(1)}, bf16[4,8,16,256]{3,2,1,0:T(8,128)(2,1)S(1)}, u32[]{:S(2)}, u32[]{:S(2)}) collective-permute-start(bf16[4,8,16,256]{3,2,1,0:T(8,128)(2,1)S(1)} %pad_maximum_fusion.2.refs_0_), channel_id=1, source_target_pairs={{0,2},{1,3},{2,4},{3,5},{4,6},{5,7},{6,0},{7,1},{8,10},{9,11},{10,... | collective-permute-start | bytes 786440 | tf_op jit(solution)/shard_map/ppermute | solution.py:36
  65.4 11.7 %collective-permute-start.18 = (bf16[4,12,16,256]{3,2,1,0:T(8,128)(2,1)S(1)}, bf16[4,12,16,256]{3,2,1,0:T(8,128)(2,1)S(1)}, u32[]{:S(2)}, u32[]{:S(2)}) collective-permute-start(bf16[4,12,16,256]{3,2,1,0:T(8,128)(2,1)S(1)} %pad_maximum_fusion.1.refs_4_), channel_id=1, source_target_pairs={{0,96},{1,97},{2,98},{3,99},{4,100},{5,101},{6,102},{7,103},{8,104... | collective-permute-start | bytes 1179656 | tf_op jit(solution)/shard_map/ppermute | solution.py:36
  65.4 17.4 %collective-permute-start.17 = (bf16[4,12,16,256]{3,2,1,0:T(8,128)(2,1)S(1)}, bf16[4,12,16,256]{3,2,1,0:T(8,128)(2,1)S(1)}, u32[]{:S(2)}, u32[]{:S(2)}) collective-permute-start(bf16[4,12,16,256]{3,2,1,0:T(8,128)(2,1)S(1)} %pad_maximum_fusion.1.refs_4_), channel_id=1, source_target_pairs={{0,64},{1,65},{2,66},{3,67},{4,68},{5,69},{6,70},{7,71},{8,72},{9,... | collective-permute-start | bytes 1179656 | tf_op jit(solution)/shard_map/ppermute | solution.py:36
  67.6 28.0 %collective-permute-start.16 = (bf16[4,12,16,256]{3,2,1,0:T(8,128)(2,1)S(1)}, bf16[4,12,16,256]{3,2,1,0:T(8,128)(2,1)S(1)}, u32[]{:S(2)}, u32[]{:S(2)}) collective-permute-start(bf16[4,12,16,256]{3,2,1,0:T(8,128)(2,1)S(1)} %pad_maximum_fusion.1.refs_4_), channel_id=1, source_target_pairs={{0,32},{1,33},{2,34},{3,35},{4,36},{5,37},{6,38},{7,39},{8,40},{9,... | collective-permute-start | bytes 1179656 | tf_op jit(solution)/shard_map/ppermute | solution.py:36
  68.7 28.5 %collective-permute-start.12 = (bf16[4,12,16,256]{3,2,1,0:T(8,128)(2,1)S(1)}, bf16[4,12,16,256]{3,2,1,0:T(8,128)(2,1)S(1)}, u32[]{:S(2)}, u32[]{:S(2)}) collective-permute-start(bf16[4,12,16,256]{3,2,1,0:T(8,128)(2,1)S(1)} %pad_maximum_fusion.refs_0_), channel_id=1, source_target_pairs={{0,6},{1,7},{2,0},{3,1},{4,2},{5,3},{6,4},{7,5},{8,14},{9,15},{10,... | collective-permute-start | bytes 1179656 | tf_op jit(solution)/shard_map/ppermute | solution.py:36
  72.8 24.6 %collective-permute-start.11 = (bf16[4,12,16,256]{3,2,1,0:T(8,128)(2,1)S(1)}, bf16[4,12,16,256]{3,2,1,0:T(8,128)(2,1)S(1)}, u32[]{:S(2)}, u32[]{:S(2)}) collective-permute-start(bf16[4,12,16,256]{3,2,1,0:T(8,128)(2,1)S(1)} %pad_maximum_fusion.refs_0_), channel_id=1, source_target_pairs={{0,4},{1,5},{2,6},{3,7},{4,0},{5,1},{6,2},{7,3},{8,12},{9,13},{10,... | collective-permute-start | bytes 1179656 | tf_op jit(solution)/shard_map/ppermute | solution.py:36
  77.1 22.7 %collective-permute-start.10 = (bf16[4,12,16,256]{3,2,1,0:T(8,128)(2,1)S(1)}, bf16[4,12,16,256]{3,2,1,0:T(8,128)(2,1)S(1)}, u32[]{:S(2)}, u32[]{:S(2)}) collective-permute-start(bf16[4,12,16,256]{3,2,1,0:T(8,128)(2,1)S(1)} %pad_maximum_fusion.refs_0_), channel_id=1, source_target_pairs={{0,2},{1,3},{2,4},{3,5},{4,6},{5,7},{6,0},{7,1},{8,10},{9,11},{10,... | collective-permute-start | bytes 1179656 | tf_op jit(solution)/shard_map/ppermute | solution.py:36
  82.8 23.6 %collective-permute-start.32 = (bf16[2,8,64,128]{3,2,1,0:T(8,128)(2,1)}, bf16[2,8,64,128]{3,2,1,0:T(8,128)(2,1)S(1)}, u32[]{:S(2)}, u32[]{:S(2)}) collective-permute-start(bf16[2,8,64,128]{3,2,1,0:T(8,128)(2,1)} %get-tuple-element.62), channel_id=1, source_target_pairs={{0,8},{1,9},{2,10},{3,11},{4,12},{5,13},{6,14},{7,15},{8,0},{9,1},... | collective-permute-start | bytes 786440 | tf_op jit(solution)/shard_map/ppermute | solution.py:36
  95.6 11.8 %collective-permute-start.33 = (bf16[2,8,64,128]{3,2,1,0:T(8,128)(2,1)}, bf16[2,8,64,128]{3,2,1,0:T(8,128)(2,1)S(1)}, u32[]{:S(2)}, u32[]{:S(2)}) collective-permute-start(bf16[2,8,64,128]{3,2,1,0:T(8,128)(2,1)} %get-tuple-element.63), channel_id=1, source_target_pairs={{0,1},{1,16},{2,3},{3,18},{4,5},{5,20},{6,7},{7,22},{8,9},{9,24},{... | collective-permute-start | bytes 786440 | tf_op jit(solution)/shard_map/ppermute | solution.py:36
  97.2 13.9 %collective-permute-start.34 = (bf16[2,8,64,128]{3,2,1,0:T(8,128)(2,1)}, bf16[2,8,64,128]{3,2,1,0:T(8,128)(2,1)S(1)}, u32[]{:S(2)}, u32[]{:S(2)}) collective-permute-start(bf16[2,8,64,128]{3,2,1,0:T(8,128)(2,1)} %get-tuple-element.64), channel_id=1, source_target_pairs={{0,9},{1,24},{2,11},{3,26},{4,13},{5,28},{6,15},{7,30},{8,1},{9,16... | collective-permute-start | bytes 786440 | tf_op jit(solution)/shard_map/ppermute | solution.py:36
  97.4 19.8 %collective-permute-start.35 = (bf16[2,8,64,128]{3,2,1,0:T(8,128)(2,1)}, bf16[2,8,64,128]{3,2,1,0:T(8,128)(2,1)S(1)}, u32[]{:S(2)}, u32[]{:S(2)}) collective-permute-start(bf16[2,8,64,128]{3,2,1,0:T(8,128)(2,1)} %get-tuple-element.65), channel_id=1, source_target_pairs={{0,16},{1,17},{2,18},{3,19},{4,20},{5,21},{6,22},{7,23},{8,24},{9,... | collective-permute-start | bytes 786440 | tf_op jit(solution)/shard_map/ppermute | solution.py:36
  105.9 29.0 %collective-permute-start.19 = (bf16[2,12,64,128]{3,2,1,0:T(8,128)(2,1)}, bf16[2,12,64,128]{3,2,1,0:T(8,128)(2,1)S(1)}, u32[]{:S(2)}, u32[]{:S(2)}) collective-permute-start(bf16[2,12,64,128]{3,2,1,0:T(8,128)(2,1)} %get-tuple-element.54), channel_id=1, source_target_pairs={{0,8},{1,9},{2,10},{3,11},{4,12},{5,13},{6,14},{7,15},{8,0},{9,1},... | collective-permute-start | bytes 1179656 | tf_op jit(solution)/shard_map/ppermute | solution.py:36
  106.4 31.2 %collective-permute-start.20 = (bf16[2,12,64,128]{3,2,1,0:T(8,128)(2,1)}, bf16[2,12,64,128]{3,2,1,0:T(8,128)(2,1)S(1)}, u32[]{:S(2)}, u32[]{:S(2)}) collective-permute-start(bf16[2,12,64,128]{3,2,1,0:T(8,128)(2,1)} %get-tuple-element.55), channel_id=1, source_target_pairs={{0,1},{1,16},{2,3},{3,18},{4,5},{5,20},{6,7},{7,22},{8,9},{9,24},{... | collective-permute-start | bytes 1179656 | tf_op jit(solution)/shard_map/ppermute | solution.py:36
  107.4 24.0 %collective-permute-start.36 = (bf16[2,8,64,128]{3,2,1,0:T(8,128)(2,1)}, bf16[2,8,64,128]{3,2,1,0:T(8,128)(2,1)S(1)}, u32[]{:S(2)}, u32[]{:S(2)}) collective-permute-start(bf16[2,8,64,128]{3,2,1,0:T(8,128)(2,1)} %get-tuple-element.66), channel_id=1, source_target_pairs={{0,24},{1,25},{2,26},{3,27},{4,28},{5,29},{6,30},{7,31},{8,16},{9,... | collective-permute-start | bytes 786440 | tf_op jit(solution)/shard_map/ppermute | solution.py:36
  111.1 20.3 %collective-permute-start.37 = (bf16[2,8,64,128]{3,2,1,0:T(8,128)(2,1)}, bf16[2,8,64,128]{3,2,1,0:T(8,128)(2,1)S(1)}, u32[]{:S(2)}, u32[]{:S(2)}) collective-permute-start(bf16[2,8,64,128]{3,2,1,0:T(8,128)(2,1)} %get-tuple-element.67), channel_id=1, source_target_pairs={{0,17},{1,0},{2,19},{3,2},{4,21},{5,4},{6,23},{7,6},{8,25},{9,8},{... | collective-permute-start | bytes 786440 | tf_op jit(solution)/shard_map/ppermute | solution.py:36
  117.1 15.2 %collective-permute-start.38 = (bf16[2,8,64,128]{3,2,1,0:T(8,128)(2,1)}, bf16[2,8,64,128]{3,2,1,0:T(8,128)(2,1)S(1)}, u32[]{:S(2)}, u32[]{:S(2)}) collective-permute-start(bf16[2,8,64,128]{3,2,1,0:T(8,128)(2,1)} %get-tuple-element.68), channel_id=1, source_target_pairs={{0,25},{1,8},{2,27},{3,10},{4,29},{5,12},{6,31},{7,14},{8,17},{9,0... | collective-permute-start | bytes 786440 | tf_op jit(solution)/shard_map/ppermute | solution.py:36
  131.4 29.2 %collective-permute-start.21 = (bf16[2,12,64,128]{3,2,1,0:T(8,128)(2,1)}, bf16[2,12,64,128]{3,2,1,0:T(8,128)(2,1)S(1)}, u32[]{:S(2)}, u32[]{:S(2)}) collective-permute-start(bf16[2,12,64,128]{3,2,1,0:T(8,128)(2,1)} %get-tuple-element.56), channel_id=1, source_target_pairs={{0,9},{1,24},{2,11},{3,26},{4,13},{5,28},{6,15},{7,30},{8,1},{9,16... | collective-permute-start | bytes 1179656 | tf_op jit(solution)/shard_map/ppermute | solution.py:36
  131.4 29.2 %collective-permute-start.22 = (bf16[2,12,64,128]{3,2,1,0:T(8,128)(2,1)}, bf16[2,12,64,128]{3,2,1,0:T(8,128)(2,1)S(1)}, u32[]{:S(2)}, u32[]{:S(2)}) collective-permute-start(bf16[2,12,64,128]{3,2,1,0:T(8,128)(2,1)} %get-tuple-element.57), channel_id=1, source_target_pairs={{0,16},{1,17},{2,18},{3,19},{4,20},{5,21},{6,22},{7,23},{8,24},{9,... | collective-permute-start | bytes 1179656 | tf_op jit(solution)/shard_map/ppermute | solution.py:36
  132.4 28.2 %collective-permute-start.23 = (bf16[2,12,64,128]{3,2,1,0:T(8,128)(2,1)}, bf16[2,12,64,128]{3,2,1,0:T(8,128)(2,1)S(1)}, u32[]{:S(2)}, u32[]{:S(2)}) collective-permute-start(bf16[2,12,64,128]{3,2,1,0:T(8,128)(2,1)} %get-tuple-element.58), channel_id=1, source_target_pairs={{0,24},{1,25},{2,26},{3,27},{4,28},{5,29},{6,30},{7,31},{8,16},{9,... | collective-permute-start | bytes 1179656 | tf_op jit(solution)/shard_map/ppermute | solution.py:36
  134.8 26.0 %collective-permute-start.24 = (bf16[2,12,64,128]{3,2,1,0:T(8,128)(2,1)}, bf16[2,12,64,128]{3,2,1,0:T(8,128)(2,1)S(1)}, u32[]{:S(2)}, u32[]{:S(2)}) collective-permute-start(bf16[2,12,64,128]{3,2,1,0:T(8,128)(2,1)} %get-tuple-element.59), channel_id=1, source_target_pairs={{0,17},{1,0},{2,19},{3,2},{4,21},{5,4},{6,23},{7,6},{8,25},{9,8},{... | collective-permute-start | bytes 1179656 | tf_op jit(solution)/shard_map/ppermute | solution.py:36
  137.6 32.0 %collective-permute-start.25 = (bf16[2,12,64,128]{3,2,1,0:T(8,128)(2,1)}, bf16[2,12,64,128]{3,2,1,0:T(8,128)(2,1)S(1)}, u32[]{:S(2)}, u32[]{:S(2)}) collective-permute-start(bf16[2,12,64,128]{3,2,1,0:T(8,128)(2,1)} %get-tuple-element.60), channel_id=1, source_target_pairs={{0,25},{1,8},{2,27},{3,10},{4,29},{5,12},{6,31},{7,14},{8,17},{9,0... | collective-permute-start | bytes 1179656 | tf_op jit(solution)/shard_map/ppermute | solution.py:36
  (52 other events, 589.5 us)

commit v2 on v1

v2 whole, which is shorter than its diff:
```python
import functools
import itertools
import math

import jax
import jax.numpy as jnp
import numpy as np
from jax import lax
from jax.experimental import pallas as pl
from jax.experimental.pallas import tpu as pltpu
from jax.sharding import PartitionSpec as P

BINS = 16
AXES = ("row", "col")
SIZES = (4, 2, 2, 4, 2)
PARTS = (2, 3)
VMEM = 63 * 1024 * 1024


def device(x, y, z, core):
    return (((x % 4 * 2 + z % 4 // 2) * 2 + core % 2) * 4 + y % 4) * 2 + z % 2


def everywhere():
    return list(itertools.product(range(4), range(4), range(4), range(2)))


LINES = [
    [device(x, y, z, core) for x in range(4) for z in range(4) for core in range(2)]
    for y in range(4)
]


def exchange(array):
    return lax.all_to_all(array, AXES, 0, 0, axis_index_groups=LINES, tiled=True)


def gather(array):
    blocks = [array]
    for k in (1, 2, 3):
        pairs = [
            (device(x, y, z, core), device(x, y + k, z, core)) for x, y, z, core in everywhere()
        ]
        blocks.append(lax.ppermute(array, AXES, pairs))
    return blocks


def split_dot(left, right, dims):
    total = None
    for _ in range(3):
        term = right.astype(jnp.bfloat16)
        right = right - term.astype(jnp.float32)
        part = lax.dot_general(left, term, dims, preferred_element_type=jnp.float32)
        total = part if total is None else total + part
    return total


def turn(phase, length):
    quarter = length // 4
    phase = phase & (length - 1)
    quadrant = lax.shift_right_logical(phase + quarter // 2, quarter.bit_length() - 1)
    angle = (phase - quadrant * quarter).astype(jnp.float32) * jnp.float32(2.0 * math.pi / length)
    square = angle * angle
    sine = angle + angle * square * (
        -1.0 / 6 + square * (1.0 / 120 + square * (-1.0 / 5040 + square * (1.0 / 362880)))
    )
    cosine = 1.0 + square * (
        -0.5 + square * (1.0 / 24 + square * (-1.0 / 720 + square * (1.0 / 40320)))
    )
    odd = (quadrant & 1) == 1
    cos_value = jnp.where(odd, sine, cosine)
    sin_value = jnp.where(odd, cosine, sine)
    cos_value = jnp.where(((quadrant + 1) & 2) == 2, -cos_value, cos_value)
    sin_value = jnp.where((quadrant & 2) == 2, -sin_value, sin_value)
    return cos_value, sin_value


def spectra_kernel(
    band_ref, whole_ref, mask_ref, map_ref, order_ref, out_ref, *scratch, length, band_count
):
    table_ref, white_ref, waves_ref, sems = scratch
    step = pl.program_id(0)
    bins = band_count * BINS
    blocks, width, _ = waves_ref.shape
    copies = [
        pltpu.make_async_copy(
            whole_ref.at[pl.ds(i * width, width)], waves_ref.at[i], sems.at[i]
        )
        for i in range(blocks)
    ]
    stations = white_ref.shape[1]
    lanes = 128

    @pl.when(step == 0)
    def _():
        for copy in copies:
            copy.start()
        row = lax.broadcasted_iota(jnp.int32, (bins, lanes), 0)
        lane = lax.broadcasted_iota(jnp.int32, (bins, lanes), 1)
        frequency = row & (BINS - 1)
        for b in range(band_count):
            first = b * BINS
            inside = (row >= first) & (row < first + BINS)
            frequency = frequency + jnp.where(inside, band_ref[b], 0)
        fine_cos, fine_sin = turn(frequency * lane, length)
        coarse_cos, coarse_sin = turn(frequency * ((lane * lanes) & (length - 1)), length)
        scaling = jnp.float32(length ** (-0.5))
        fine_cos = fine_cos * scaling
        fine_sin = fine_sin * scaling
        for part in range(length // lanes):
            c = coarse_cos[:, part : part + 1]
            s = coarse_sin[:, part : part + 1]
            columns = slice(part * lanes, (part + 1) * lanes)
            table_ref[:bins, columns] = (c * fine_cos - s * fine_sin).astype(jnp.bfloat16)
            table_ref[bins:, columns] = (-s * fine_cos - c * fine_sin).astype(jnp.bfloat16)

    for i in range(blocks):
        pl.when(step == i)(copies[i].wait)
    wave_ref = waves_ref.at[step]
    spectra = lax.dot_general(
        table_ref[...], wave_ref[...], (((1,), (1,)), ((), ())), preferred_element_type=jnp.float32
    )
    squares = jnp.zeros((width, lanes), jnp.float32)
    for part in range(length // lanes):
        piece = wave_ref[:, part * lanes : (part + 1) * lanes].astype(jnp.float32)
        squares = squares + piece * piece
    ones = jnp.ones((8, lanes), jnp.bfloat16)
    total = split_dot(ones, squares, (((1,), (1,)), ((), ())))[:1]
    inverse = lax.rsqrt(total / length + 1e-06)
    real_part = spectra[:bins] * inverse
    imag_part = spectra[bins:] * inverse
    power = real_part * real_part + imag_part * imag_part
    banded = power.reshape(band_count, BINS, width)
    mean = jnp.broadcast_to(jnp.mean(banded, axis=1, keepdims=True), banded.shape)
    mask = mask_ref[...].astype(jnp.float32)
    factor = mask * lax.rsqrt(power + mean.reshape(bins, width) + 0.1)
    columns = pl.ds(pl.multiple_of(step * width, width), width)
    white_ref[:bins, columns] = (real_part * factor).astype(jnp.bfloat16)
    white_ref[bins:, columns] = (imag_part * factor).astype(jnp.bfloat16)

    @pl.when(step == pl.num_programs(0) - 1)
    def _():
        devices, share = out_ref.shape[0], out_ref.shape[1] * lanes // stations
        sorted_rows = jnp.dot(
            order_ref[...], white_ref[...], preferred_element_type=jnp.float32
        ).astype(jnp.bfloat16)
        block = 2 * lanes
        for first in range(0, stations, block):
            station = lax.broadcasted_iota(jnp.int32, (stations, block), 0)
            take = station == map_ref[:, first : first + block]
            take = take.astype(jnp.float32).astype(jnp.bfloat16)
            moved = jnp.dot(sorted_rows, take, preferred_element_type=jnp.float32)
            moved = moved.astype(jnp.bfloat16)
            for goal_device in range(devices):
                piece = moved[goal_device * share : (goal_device + 1) * share]
                for side in range(2):
                    row = (first // lanes + side) * share
                    out_ref[goal_device, row : row + share] = piece[
                        :, side * lanes : (side + 1) * lanes
                    ]


def make_spectra(waveform, valid_mask, band_starts, station_map, devices):
    stations, length = waveform.shape
    band_count = band_starts.shape[0]
    rows = 2 * BINS * band_count
    width = 256
    bins = rows // 2
    order = np.arange(rows).reshape(2, devices, bins // devices).transpose(1, 0, 2).reshape(-1)
    order = jnp.asarray(np.eye(rows, dtype=np.float32)[order], jnp.bfloat16)
    shape = (devices, rows // devices * stations // 128, 128)
    smem = pl.BlockSpec(memory_space=pltpu.SMEM)
    return pl.pallas_call(
        functools.partial(spectra_kernel, length=length, band_count=band_count),
        grid=(stations // width,),
        in_specs=[
            smem,
            pl.BlockSpec(memory_space=pl.ANY),
            pl.BlockSpec((1, width), lambda i: (0, i)),
            pl.BlockSpec((1, stations), lambda i: (0, 0)),
            pl.BlockSpec((rows, rows), lambda i: (0, 0)),
        ],
        out_specs=pl.BlockSpec(shape, lambda i: (0, 0, 0)),
        out_shape=jax.ShapeDtypeStruct(shape, jnp.bfloat16),
        scratch_shapes=[
            pltpu.VMEM((rows, length), jnp.bfloat16),
            pltpu.VMEM((rows, stations), jnp.bfloat16),
            pltpu.VMEM((stations // width, width, length), jnp.bfloat16),
            pltpu.SemaphoreType.DMA((stations // width,)),
        ],
        compiler_params=pltpu.CompilerParams(vmem_limit_bytes=VMEM),
        cost_estimate=pl.CostEstimate(
            flops=2 * rows * length * stations, bytes_accessed=2 * stations * length, transcendentals=0
        ),
        name="spectra",
    )(band_starts, waveform, valid_mask, station_map, order)


def weave_kernel(in_ref, *outs):
    lanes = in_ref.shape[2]
    stations = outs[0].shape[3]
    share = in_ref.shape[1] * lanes // stations
    woven = jnp.swapaxes(in_ref[...].astype(jnp.float32), 0, 1).astype(jnp.bfloat16)
    for block in range(stations // lanes):
        for part in range(2):
            row = block * share + part * share // 2
            for out in outs:
                for j in range(out.shape[1]):
                    out[part, j, :, block * lanes : (block + 1) * lanes] = woven[row]
                    row += 1


def weave(array, stations):
    whole = pl.BlockSpec(memory_space=pltpu.VMEM)
    windows = array.shape[0]
    shapes = [jax.ShapeDtypeStruct((2, nb, windows, stations), jnp.bfloat16) for nb in PARTS]
    return pl.pallas_call(
        weave_kernel,
        in_specs=[whole],
        out_specs=[whole] * len(shapes),
        out_shape=shapes,
        compiler_params=pltpu.CompilerParams(vmem_limit_bytes=VMEM),
        name="weave",
    )(array)


def product_kernel(y_ref, *refs, scaling):
    blocks, out = refs[:4], refs[4]
    width = 256
    columns = pl.ds(pl.multiple_of(y_ref[0] * width, width), width)
    pieces = [(block, part) for part in range(2) for block in blocks]
    left = jnp.concatenate([block[part, 0] for block, part in pieces], axis=0)
    right = [block[part, 0, :, columns] for block, part in pieces]
    turned = right[4:] + [-piece for piece in right[:4]]
    both = jnp.concatenate(
        [jnp.concatenate(right, axis=0), jnp.concatenate(turned, axis=0)], axis=1
    )
    dims = (((0,), (0,)), ((), ()))
    result = lax.dot_general(left, both, dims, preferred_element_type=jnp.float32)
    result = (result * scaling).astype(jnp.bfloat16)
    for group in range(out.shape[0]):
        first_row = group // 8 * 256 + group // 4 % 2 * 128 + group % 2 * 64
        for part in range(2):
            first_col = part * width + group // 2 % 2 * 128
            out[group, part, 0] = result[first_row : first_row + 64, first_col : first_col + 128]


def product(y, blocks, scaling, devices):
    _, nb, windows, stations = blocks[0].shape
    spec = pl.BlockSpec((2, 1, windows, stations), lambda i: (0, i, 0, 0))
    return pl.pallas_call(
        functools.partial(product_kernel, scaling=scaling),
        grid=(nb,),
        in_specs=[pl.BlockSpec(memory_space=pltpu.SMEM)] + [spec] * 4,
        out_specs=pl.BlockSpec((devices, 2, 1, 64, 128), lambda i: (0, 0, i, 0, 0)),
        out_shape=jax.ShapeDtypeStruct((devices, 2, nb, 64, 128), jnp.bfloat16),
        compiler_params=pltpu.CompilerParams(vmem_limit_bytes=VMEM),
        cost_estimate=pl.CostEstimate(
            flops=nb * 2**28, bytes_accessed=nb * 2**21, transcendentals=0
        ),
        name="product",
    )(y, *blocks)


def place_kernel(in_ref, *refs, start, stride):
    out, buffer, in_sems, out_sems = refs[-4:]
    devices, _, nb = buffer.shape[:3]
    arrivals = [
        pltpu.make_async_copy(in_ref.at[i], buffer.at[i], in_sems.at[i]) for i in range(devices)
    ]
    departures = [
        pltpu.make_async_copy(
            buffer.at[i], out.at[:, pl.ds(start + i * stride, nb)], out_sems.at[i]
        )
        for i in range(devices)
    ]
    for arrival in arrivals:
        arrival.start()
    for arrival, departure in zip(arrivals, departures):
        arrival.wait()
        departure.start()
    for departure in departures:
        departure.wait()


def place_blocks(array, total, start, stride, shape):
    anywhere = pl.BlockSpec(memory_space=pl.ANY)
    operands = [array] + ([] if total is None else [total])
    devices = array.shape[0]
    return pl.pallas_call(
        functools.partial(place_kernel, start=start, stride=stride),
        in_specs=[anywhere] * len(operands),
        out_specs=anywhere,
        out_shape=shape,
        scratch_shapes=[
            pltpu.VMEM(array.shape, array.dtype),
            pltpu.SemaphoreType.DMA((devices,)),
            pltpu.SemaphoreType.DMA((devices,)),
        ],
        input_output_aliases={} if total is None else {1: 0},
        compiler_params=pltpu.CompilerParams(vmem_limit_bytes=VMEM),
        name="place",
    )(*operands)


def body(waveform, valid_mask, band_starts, station_map):
    y = (lax.axis_index("col") // 2).astype(jnp.int32).reshape(1)
    stations = waveform.shape[1]
    windows = waveform.shape[0] * lax.axis_size("row") * lax.axis_size("col")
    bins = BINS * band_starts.shape[0]
    scaling = float(windows) ** (-0.5)
    devices = len(LINES[0])
    spectra = make_spectra(
        waveform[0], valid_mask, band_starts, station_map.reshape(1, stations), devices
    )
    woven = weave(exchange(spectra), stations)
    shape = jax.ShapeDtypeStruct((2, bins, 64, 128), jnp.bfloat16)
    total = None
    start = 0
    for part in woven:
        blocks = exchange(product(y, gather(part), scaling, devices))
        total = place_blocks(blocks, total, start, sum(PARTS), shape)
        start += part.shape[1]
    return total


def solution(mesh):
    placed = (P(AXES, None, None), P(AXES, None), P(), P())
    return jax.shard_map(
        body, mesh=mesh, in_specs=placed, out_specs=P(None, None, "row", "col"), check_vma=False
    )
```

time: 175 us -> 147 us (0.84)
  the two profiles are of different devices: /device:TPU:15 before, /device:TPU:1 now
where the time goes in v2:
time: 147 us; the launch traced here: 146 us
  waiting for transfers between devices  72.9 us (50%)
  Pallas kernels  33.7 us (23%)
  blocking collectives  22.5 us (15%)
  starting transfers between devices  15.7 us (11%)
    all_to_all x2, waiting for transfers between devices, exchange(): lax.all_to_all(array, AXES, 0, 0, axis_index_groups=LINES, tiled=True)  39.2 us
    ppermute x6, waiting for transfers between devices, gather(): blocks.append(lax.ppermute(array, AXES, pairs))  33.7 us
    all_to_all x1, blocking collectives, exchange(): lax.all_to_all(array, AXES, 0, 0, axis_index_groups=LINES, tiled=True)  22.5 us
    pallas_call x1, Pallas kernels, make_spectra(): pl.pallas_call(functools.partial(spectra_kernel, length=length, band_coun...  17.2 us
    all_to_all x2, starting transfers between devices, exchange(): lax.all_to_all(array, AXES, 0, 0, axis_index_groups=LINES, tiled=True)  10.4 us
    pallas_call x2, Pallas kernels, product(): pl.pallas_call(functools.partial(product_kernel, scaling=scaling), grid=(...  7.94 us
    pallas_call x2, Pallas kernels, place_blocks(): pl.pallas_call(functools.partial(place_kernel, start=start, stride=stride...  6.29 us
    ppermute x6, starting transfers between devices, gather(): blocks.append(lax.ppermute(array, AXES, pairs))  5.36 us
  transfers between devices with their start and end apart: 8, of which 7 were waited for; matrix products, arithmetic and copies ran while one was open for 0% of the time, Pallas kernels for 5%

profile of v2, /device:TPU:1, one launch (start us, length us, event | category | flops | bytes accessed | tf_op | source)
XLA Modules:
  0.0 146.3 jit_solution(17862083901297277553)
XLA Ops:
  0.0 17.2 %spectra.1 = bf16[32,80,128]{2,1,0:T(8,128)(2,1)} custom-call(s32[10]{0:T(128)} %band_ref.1, bf16[1024,8192]{1,0:T(8,128)(2,1)} %bitcast.3, s32[1,1024]{1,0:T(1,128)} %mask_ref.1, s32[1,1024]{1,0:T(1,128)} %bitcast.4, bf16[320,320]{1,0:T(8,128)(2,1)} %constant.20.clone.order_ref), custom_call_target="tpu_custom_call" | custom-call | flops 5368709120 | bytes 16777216 | tf_op jit(solution)/shard_map/spectra/pallas_call | solution.py:173
  17.2 22.5 %all_to_all.15.in_ref = bf16[32,80,128]{2,1,0:T(8,128)(2,1)} all-to-all(bf16[32,80,128]{2,1,0:T(8,128)(2,1)} %spectra.1), channel_id=1, replica_groups={{0,8,1,9,16,24,17,25,32,40,33,41,48,56,49,57,64,72,65,73,80,88,81,89,96..., dimensions={0} | all-to-all | bytes 1310720 | tf_op jit(solution)/shard_map/all_to_all | solution.py:35
  39.7 2.3 %weave.1 = (bf16[2,2,32,1024]{3,2,1,0:T(8,128)(2,1)}, bf16[2,3,32,1024]{3,2,1,0:T(8,128)(2,1)}) custom-call(bf16[32,80,128]{2,1,0:T(8,128)(2,1)} %all_to_all.15.in_ref), custom_call_target="tpu_custom_call" | custom-call | tf_op jit(solution)/shard_map/weave/pallas_call | solution.py:217
  42.0 2.8 %collective-permute-start.5 = (bf16[2,2,32,1024]{3,2,1,0:T(8,128)(2,1)}, bf16[2,2,32,1024]{3,2,1,0:T(8,128)(2,1)S(1)}, u32[]{:S(2)}, u32[]{:S(2)}) collective-permute-start(bf16[2,2,32,1024]{3,2,1,0:T(8,128)(2,1)} %get-tuple-element.8.refs_0_), channel_id=1, source_target_pairs={{0,6},{8,14},{1,7},{9,15},{16,22},{24,30},{17,23},{25,31},{2,0},{1... | collective-permute-start | bytes 786440 | tf_op jit(solution)/shard_map/ppermute | solution.py:44
  44.7 0.4 collective-permute-start.4
  45.1 0.7 collective-permute-start.3
  45.8 10.6 %collective-permute-done.5.refs_3_ = bf16[2,2,32,1024]{3,2,1,0:T(8,128)(2,1)S(1)} collective-permute-done((bf16[2,2,32,1024]{3,2,1,0:T(8,128)(2,1)}, bf16[2,2,32,1024]{3,2,1,0:T(8,128)(2,1)S(1)}, u32[]{:S(2)}, u32[]{:S(2)}) %collective-permute-start.5) | collective-permute-done | bytes 262176 | tf_op jit(solution)/shard_map/ppermute | solution.py:44
  56.4 4.0 %collective-permute-done.3.refs_1_ = bf16[2,2,32,1024]{3,2,1,0:T(8,128)(2,1)S(1)} collective-permute-done((bf16[2,2,32,1024]{3,2,1,0:T(8,128)(2,1)}, bf16[2,2,32,1024]{3,2,1,0:T(8,128)(2,1)S(1)}, u32[]{:S(2)}, u32[]{:S(2)}) %collective-permute-start.3) | collective-permute-done | bytes 262176 | tf_op jit(solution)/shard_map/ppermute | solution.py:44
  60.3 0.7 copy-done.5
  61.0 3.1 %product.3 = bf16[32,2,2,64,128]{4,3,2,1,0:T(8,128)(2,1)} custom-call(s32[1]{0:T(128)} %bitcast.y_ref, bf16[2,2,32,1024]{3,2,1,0:T(8,128)(2,1)} %get-tuple-element.8.refs_0_, bf16[2,2,32,1024]{3,2,1,0:T(8,128)(2,1)} %copy-done.5, bf16[2,2,32,1024]{3,2,1,0:T(8,128)(2,1)} %copy-done.4, bf16[2,2,32,1024]{3,2,1,0:T(8,128)(2,1)} %copy-done.3), custom_call_target="tpu_custom_call" | custom-call | flops 536870912 | bytes 4194304 | tf_op jit(solution)/shard_map/product/pallas_call | solution.py:251
  64.2 4.8 %all-to-all-start.2 = ((bf16[32,2,2,64,128]{4,3,2,1,0:T(8,128)(2,1)}), bf16[32,2,2,64,128]{4,3,2,1,0:T(8,128)(2,1)}, u32[]{:S(2)}, u32[]{:S(2)}) async-start(bf16[32,2,2,64,128]{4,3,2,1,0:T(8,128)(2,1)} %product.3), calls=%async_computation.2 | async-start | bytes 4194304 | tf_op jit(solution)/shard_map/all_to_all | solution.py:35
  69.0 0.4 collective-permute-start.2
  69.4 0.3 collective-permute-start.1
  69.7 0.8 collective-permute-start
  70.5 8.9 %collective-permute-done.2.refs_3_ = bf16[2,3,32,1024]{3,2,1,0:T(8,128)(2,1)S(1)} collective-permute-done((bf16[2,3,32,1024]{3,2,1,0:T(8,128)(2,1)S(1)}, bf16[2,3,32,1024]{3,2,1,0:T(8,128)(2,1)S(1)}, u32[]{:S(2)}, u32[]{:S(2)}) %collective-permute-start.2) | collective-permute-done | bytes 393248 | tf_op jit(solution)/shard_map/ppermute | solution.py:44
  79.4 1.6 %collective-permute-done.1.refs_2_ = bf16[2,3,32,1024]{3,2,1,0:T(8,128)(2,1)S(1)} collective-permute-done((bf16[2,3,32,1024]{3,2,1,0:T(8,128)(2,1)S(1)}, bf16[2,3,32,1024]{3,2,1,0:T(8,128)(2,1)S(1)}, u32[]{:S(2)}, u32[]{:S(2)}) %collective-permute-start.1) | collective-permute-done | bytes 393248 | tf_op jit(solution)/shard_map/ppermute | solution.py:44
  81.0 0.7 copy-done.2
  81.7 8.7 %collective-permute-done.refs_1_ = bf16[2,3,32,1024]{3,2,1,0:T(8,128)(2,1)} collective-permute-done((bf16[2,3,32,1024]{3,2,1,0:T(8,128)(2,1)S(1)}, bf16[2,3,32,1024]{3,2,1,0:T(8,128)(2,1)}, u32[]{:S(2)}, u32[]{:S(2)}) %collective-permute-start) | collective-permute-done | bytes 393248 | tf_op jit(solution)/shard_map/ppermute | solution.py:44
  90.5 4.8 %product.2 = bf16[32,2,3,64,128]{4,3,2,1,0:T(8,128)(2,1)} custom-call(s32[1]{0:T(128)} %bitcast.y_ref, bf16[2,3,32,1024]{3,2,1,0:T(8,128)(2,1)} %get-tuple-element.7.refs_0_, bf16[2,3,32,1024]{3,2,1,0:T(8,128)(2,1)} %collective-permute-done.refs_1_, bf16[2,3,32,1024]{3,2,1,0:T(8,128)(2,1)} %copy-done.2, bf16[2,3,32,1024]{3,2,1,0:T(8,128)(2,1)} %copy-done.1), custom_call_target="tpu_custom_call" | custom-call | flops 805306368 | bytes 6291456 | tf_op jit(solution)/shard_map/product/pallas_call | solution.py:251
  95.3 2.1 %all-to-all-done.2.in_ref = bf16[32,2,2,64,128]{4,3,2,1,0:T(8,128)(2,1)} async-done(((bf16[32,2,2,64,128]{4,3,2,1,0:T(8,128)(2,1)}), bf16[32,2,2,64,128]{4,3,2,1,0:T(8,128)(2,1)}, u32[]{:S(2)}, u32[]{:S(2)}) %all-to-all-start.2) | async-done | bytes 2097184 | tf_op jit(solution)/shard_map/all_to_all | solution.py:35
  97.4 5.6 %all-to-all-start.1 = ((bf16[32,2,3,64,128]{4,3,2,1,0:T(8,128)(2,1)}), bf16[32,2,3,64,128]{4,3,2,1,0:T(8,128)(2,1)}, u32[]{:S(2)}, u32[]{:S(2)}) async-start(bf16[32,2,3,64,128]{4,3,2,1,0:T(8,128)(2,1)} %product.2), calls=%async_computation.1 | async-start | bytes 6291456 | tf_op jit(solution)/shard_map/all_to_all | solution.py:35
  103.0 2.8 %place.2.refs_0_ = bf16[2,160,64,128]{3,2,1,0:T(8,128)(2,1)} custom-call(bf16[32,2,2,64,128]{4,3,2,1,0:T(8,128)(2,1)} %all-to-all-done.2.in_ref), custom_call_target="tpu_custom_call" | custom-call | tf_op jit(solution)/shard_map/place/pallas_call | solution.py:290
  105.8 37.0 %all-to-all-done.1.in_ref = bf16[32,2,3,64,128]{4,3,2,1,0:T(8,128)(2,1)} async-done(((bf16[32,2,3,64,128]{4,3,2,1,0:T(8,128)(2,1)}), bf16[32,2,3,64,128]{4,3,2,1,0:T(8,128)(2,1)}, u32[]{:S(2)}, u32[]{:S(2)}) %all-to-all-start.1) | async-done | bytes 3145760 | tf_op jit(solution)/shard_map/all_to_all | solution.py:35
  142.8 3.5 %place.3 = bf16[2,160,64,128]{3,2,1,0:T(8,128)(2,1)} custom-call(bf16[32,2,3,64,128]{4,3,2,1,0:T(8,128)(2,1)} %all-to-all-done.1.in_ref, bf16[2,160,64,128]{3,2,1,0:T(8,128)(2,1)} %place.2.refs_0_), custom_call_target="tpu_custom_call", output_to_operand_aliasing={{}: (1, {})} | custom-call | tf_op jit(solution)/shard_map/place/pallas_call | solution.py:290
  (11 shorter events, 0.0 us)
Async XLA Ops:
  42.0 14.4 %collective-permute-start.5 = (bf16[2,2,32,1024]{3,2,1,0:T(8,128)(2,1)}, bf16[2,2,32,1024]{3,2,1,0:T(8,128)(2,1)S(1)}, u32[]{:S(2)}, u32[]{:S(2)}) collective-permute-start(bf16[2,2,32,1024]{3,2,1,0:T(8,128)(2,1)} %get-tuple-element.8.refs_0_), channel_id=1, source_target_pairs={{0,6},{8,14},{1,7},{9,15},{16,22},{24,30},{17,23},{25,31},{2,0},{1... | collective-permute-start | bytes 786440 | tf_op jit(solution)/shard_map/ppermute | solution.py:44
  44.7 11.6 %collective-permute-start.4 = (bf16[2,2,32,1024]{3,2,1,0:T(8,128)(2,1)}, bf16[2,2,32,1024]{3,2,1,0:T(8,128)(2,1)S(1)}, u32[]{:S(2)}, u32[]{:S(2)}) collective-permute-start(bf16[2,2,32,1024]{3,2,1,0:T(8,128)(2,1)} %get-tuple-element.8.refs_0_), channel_id=1, source_target_pairs={{0,4},{8,12},{1,5},{9,13},{16,20},{24,28},{17,21},{25,29},{2,6},{1... | collective-permute-start | bytes 786440 | tf_op jit(solution)/shard_map/ppermute | solution.py:44
  45.1 15.2 %collective-permute-start.3 = (bf16[2,2,32,1024]{3,2,1,0:T(8,128)(2,1)}, bf16[2,2,32,1024]{3,2,1,0:T(8,128)(2,1)S(1)}, u32[]{:S(2)}, u32[]{:S(2)}) collective-permute-start(bf16[2,2,32,1024]{3,2,1,0:T(8,128)(2,1)} %get-tuple-element.8.refs_0_), channel_id=1, source_target_pairs={{0,2},{8,10},{1,3},{9,11},{16,18},{24,26},{17,19},{25,27},{2,4},{1... | collective-permute-start | bytes 786440 | tf_op jit(solution)/shard_map/ppermute | solution.py:44
  56.4 4.7 %copy-start.3 = (bf16[2,2,32,1024]{3,2,1,0:T(8,128)(2,1)}, bf16[2,2,32,1024]{3,2,1,0:T(8,128)(2,1)S(1)}, u32[]{:S(2)}) copy-start(bf16[2,2,32,1024]{3,2,1,0:T(8,128)(2,1)S(1)} %collective-permute-done.5.refs_3_) | copy-start | bytes 786436
  56.4 4.7 %copy-start.4 = (bf16[2,2,32,1024]{3,2,1,0:T(8,128)(2,1)}, bf16[2,2,32,1024]{3,2,1,0:T(8,128)(2,1)S(1)}, u32[]{:S(2)}) copy-start(bf16[2,2,32,1024]{3,2,1,0:T(8,128)(2,1)S(1)} %collective-permute-done.4.refs_2_) | copy-start | bytes 786436
  60.3 0.7 copy-start.5
  61.0 7.9 %copy-start = (bf16[2,3,32,1024]{3,2,1,0:T(8,128)(2,1)S(1)}, bf16[2,3,32,1024]{3,2,1,0:T(8,128)(2,1)}, u32[]{:S(2)}) copy-start(bf16[2,3,32,1024]{3,2,1,0:T(8,128)(2,1)} %get-tuple-element.7.refs_0_) | copy-start | bytes 1179652
  64.2 33.2 %all-to-all-start.2 = ((bf16[32,2,2,64,128]{4,3,2,1,0:T(8,128)(2,1)}), bf16[32,2,2,64,128]{4,3,2,1,0:T(8,128)(2,1)}, u32[]{:S(2)}, u32[]{:S(2)}) async-start(bf16[32,2,2,64,128]{4,3,2,1,0:T(8,128)(2,1)} %product.3), calls=%async_computation.2 | async-start | bytes 4194304 | tf_op jit(solution)/shard_map/all_to_all | solution.py:35
  69.0 10.4 %collective-permute-start.2 = (bf16[2,3,32,1024]{3,2,1,0:T(8,128)(2,1)S(1)}, bf16[2,3,32,1024]{3,2,1,0:T(8,128)(2,1)S(1)}, u32[]{:S(2)}, u32[]{:S(2)}) collective-permute-start(bf16[2,3,32,1024]{3,2,1,0:T(8,128)(2,1)S(1)} %copy-done), channel_id=1, source_target_pairs={{0,6},{8,14},{1,7},{9,15},{16,22},{24,30},{17,23},{25,31},{2,0},{1... | collective-permute-start | bytes 1179656 | tf_op jit(solution)/shard_map/ppermute | solution.py:44
  69.4 11.6 %collective-permute-start.1 = (bf16[2,3,32,1024]{3,2,1,0:T(8,128)(2,1)S(1)}, bf16[2,3,32,1024]{3,2,1,0:T(8,128)(2,1)S(1)}, u32[]{:S(2)}, u32[]{:S(2)}) collective-permute-start(bf16[2,3,32,1024]{3,2,1,0:T(8,128)(2,1)S(1)} %copy-done), channel_id=1, source_target_pairs={{0,4},{8,12},{1,5},{9,13},{16,20},{24,28},{17,21},{25,29},{2,6},{1... | collective-permute-start | bytes 1179656 | tf_op jit(solution)/shard_map/ppermute | solution.py:44
  69.7 20.7 %collective-permute-start = (bf16[2,3,32,1024]{3,2,1,0:T(8,128)(2,1)S(1)}, bf16[2,3,32,1024]{3,2,1,0:T(8,128)(2,1)}, u32[]{:S(2)}, u32[]{:S(2)}) collective-permute-start(bf16[2,3,32,1024]{3,2,1,0:T(8,128)(2,1)S(1)} %copy-done), channel_id=1, source_target_pairs={{0,2},{8,10},{1,3},{9,11},{16,18},{24,26},{17,19},{25,27},{2,4},{1... | collective-permute-start | bytes 1179656 | tf_op jit(solution)/shard_map/ppermute | solution.py:44
  79.4 11.0 %copy-start.1 = (bf16[2,3,32,1024]{3,2,1,0:T(8,128)(2,1)}, bf16[2,3,32,1024]{3,2,1,0:T(8,128)(2,1)S(1)}, u32[]{:S(2)}) copy-start(bf16[2,3,32,1024]{3,2,1,0:T(8,128)(2,1)S(1)} %collective-permute-done.2.refs_3_) | copy-start | bytes 1179652
  81.0 0.7 copy-start.2
  97.4 45.4 %all-to-all-start.1 = ((bf16[32,2,3,64,128]{4,3,2,1,0:T(8,128)(2,1)}), bf16[32,2,3,64,128]{4,3,2,1,0:T(8,128)(2,1)}, u32[]{:S(2)}, u32[]{:S(2)}) async-start(bf16[32,2,3,64,128]{4,3,2,1,0:T(8,128)(2,1)} %product.2), calls=%async_computation.1 | async-start | bytes 6291456 | tf_op jit(solution)/shard_map/all_to_all | solution.py:35

commit v3 on v2

--- a/solution.py
+++ b/solution.py
@@ -21,28 +21,40 @@
     return (((x % 4 * 2 + z % 4 // 2) * 2 + core % 2) * 4 + y % 4) * 2 + z % 2
 
 
-def everywhere():
-    return list(itertools.product(range(4), range(4), range(4), range(2)))
-
-
-LINES = [
-    [device(x, y, z, core) for x in range(4) for z in range(4) for core in range(2)]
-    for y in range(4)
+PLANES = [
+    [device(x, y, z, 0) for x in range(4) for z in range(4)] for y in range(4)
+] + [
+    [device(x, y, z, 1) for y in range(4) for z in range(4)] for x in range(4)
 ]
 
 
+def own_place():
+    row, col = lax.axis_index("row"), lax.axis_index("col")
+    core = row % 2
+    return core, core * (row // 4) + (1 - core) * (col // 2)
+
+
 def exchange(array):
-    return lax.all_to_all(array, AXES, 0, 0, axis_index_groups=LINES, tiled=True)
+    return lax.all_to_all(array, AXES, 0, 0, axis_index_groups=PLANES, tiled=True)
+
+
+def permute(array, move):
+    pairs = [
+        (device(*place), device(*move(*place)))
+        for place in itertools.product(range(4), range(4), range(4), range(2))
+    ]
+    return lax.ppermute(array, AXES, pairs)
+
+
+def swap(array):
+    return permute(array, lambda x, y, z, core: (x, y, z, core + 1))
 
 
 def gather(array):
-    blocks = [array]
-    for k in (1, 2, 3):
-        pairs = [
-            (device(x, y, z, core), device(x, y + k, z, core)) for x, y, z, core in everywhere()
-        ]
-        blocks.append(lax.ppermute(array, AXES, pairs))
-    return blocks
+    return [array] + [
+        permute(array, lambda x, y, z, core: (x + k * core, y + k * (1 - core), z, core))
+        for k in (1, 2, 3)
+    ]
 
 
 def split_dot(left, right, dims):
@@ -76,9 +88,10 @@
 
 
 def spectra_kernel(
-    band_ref, whole_ref, mask_ref, map_ref, order_ref, out_ref, *scratch, length, band_count
+    band_ref, whole_ref, mask_ref, map_ref, order_ref, *refs, length, band_count
 ):
-    table_ref, white_ref, waves_ref, sems = scratch
+    outs = refs[:2]
+    table_ref, white_ref, waves_ref, sems = refs[2:]
     step = pl.program_id(0)
     bins = band_count * BINS
     blocks, width, _ = waves_ref.shape
@@ -107,12 +120,19 @@
         scaling = jnp.float32(length ** (-0.5))
         fine_cos = fine_cos * scaling
         fine_sin = fine_sin * scaling
-        for part in range(length // lanes):
+        odd = (frequency & 1) == 1
+        half = length // 2
+        for part in range(half // lanes):
             c = coarse_cos[:, part : part + 1]
             s = coarse_sin[:, part : part + 1]
-            columns = slice(part * lanes, (part + 1) * lanes)
-            table_ref[:bins, columns] = (c * fine_cos - s * fine_sin).astype(jnp.bfloat16)
-            table_ref[bins:, columns] = (-s * fine_cos - c * fine_sin).astype(jnp.bfloat16)
+            real_part = c * fine_cos - s * fine_sin
+            imag_part = -s * fine_cos - c * fine_sin
+            first = part * lanes
+            near, far = slice(first, first + lanes), slice(half + first, half + first + lanes)
+            table_ref[:bins, near] = real_part.astype(jnp.bfloat16)
+            table_ref[bins:, near] = imag_part.astype(jnp.bfloat16)
+            table_ref[:bins, far] = jnp.where(odd, -real_part, real_part).astype(jnp.bfloat16)
+            table_ref[bins:, far] = jnp.where(odd, -imag_part, imag_part).astype(jnp.bfloat16)
 
     for i in range(blocks):
         pl.when(step == i)(copies[i].wait)
@@ -140,9 +160,8 @@
 
     @pl.when(step == pl.num_programs(0) - 1)
     def _():
-        devices, share = out_ref.shape[0], out_ref.shape[1] * lanes // stations
         sorted_rows = jnp.dot(
-            order_ref[...], white_ref[...], preferred_element_type=jnp.float32
+            order_ref[own_place()[0]], white_ref[...], preferred_element_type=jnp.float32
         ).astype(jnp.bfloat16)
         block = 2 * lanes
         for first in range(0, stations, block):
@@ -151,13 +170,15 @@
             take = take.astype(jnp.float32).astype(jnp.bfloat16)
             moved = jnp.dot(sorted_rows, take, preferred_element_type=jnp.float32)
             moved = moved.astype(jnp.bfloat16)
-            for goal_device in range(devices):
-                piece = moved[goal_device * share : (goal_device + 1) * share]
-                for side in range(2):
-                    row = (first // lanes + side) * share
-                    out_ref[goal_device, row : row + share] = piece[
-                        :, side * lanes : (side + 1) * lanes
-                    ]
+            count = 0
+            for out in outs:
+                share = out.shape[1] * lanes // stations
+                for goal in range(out.shape[0]):
+                    piece = moved[count : count + share]
+                    for side in range(2):
+                        row = (first // lanes + side) * share
+                        out[goal, row : row + share] = piece[:, side * lanes : (side + 1) * lanes]
+                    count += share
 
 
 def make_spectra(waveform, valid_mask, band_starts, station_map, devices):
@@ -165,10 +186,18 @@
     band_count = band_starts.shape[0]
     rows = 2 * BINS * band_count
     width = 256
-    bins = rows // 2
-    order = np.arange(rows).reshape(2, devices, bins // devices).transpose(1, 0, 2).reshape(-1)
+    halves = []
+    for half in range(2):
+        first = half * rows // 4
+        pieces = []
+        for nb in PARTS:
+            pieces.append(np.arange(first, first + nb * devices).reshape(devices, 1, nb))
+            first += nb * devices
+        both = np.concatenate(pieces, axis=2) + np.array([[0], [rows // 2]])
+        halves.append(both.reshape(-1))
+    order = np.stack([np.concatenate(halves), np.concatenate(halves[::-1])])
     order = jnp.asarray(np.eye(rows, dtype=np.float32)[order], jnp.bfloat16)
-    shape = (devices, rows // devices * stations // 128, 128)
+    shape = (devices, rows // 2 // devices * stations // 128, 128)
     smem = pl.BlockSpec(memory_space=pltpu.SMEM)
     return pl.pallas_call(
         functools.partial(spectra_kernel, length=length, band_count=band_count),
@@ -178,10 +207,10 @@
             pl.BlockSpec(memory_space=pl.ANY),
             pl.BlockSpec((1, width), lambda i: (0, i)),
             pl.BlockSpec((1, stations), lambda i: (0, 0)),
-            pl.BlockSpec((rows, rows), lambda i: (0, 0)),
+            pl.BlockSpec((2, rows, rows), lambda i: (0, 0, 0)),
         ],
-        out_specs=pl.BlockSpec(shape, lambda i: (0, 0, 0)),
-        out_shape=jax.ShapeDtypeStruct(shape, jnp.bfloat16),
+        out_specs=[pl.BlockSpec(shape, lambda i: (0, 0, 0))] * 2,
+        out_shape=[jax.ShapeDtypeStruct(shape, jnp.bfloat16)] * 2,
         scratch_shapes=[
             pltpu.VMEM((rows, length), jnp.bfloat16),
             pltpu.VMEM((rows, stations), jnp.bfloat16),
@@ -224,78 +253,109 @@
     )(array)
 
 
-def product_kernel(y_ref, *refs, scaling):
+def product_kernel(*refs, scaling):
     blocks, out = refs[:4], refs[4]
+    core, block = own_place()
     width = 256
-    columns = pl.ds(pl.multiple_of(y_ref[0] * width, width), width)
-    pieces = [(block, part) for part in range(2) for block in blocks]
-    left = jnp.concatenate([block[part, 0] for block, part in pieces], axis=0)
-    right = [block[part, 0, :, columns] for block, part in pieces]
-    turned = right[4:] + [-piece for piece in right[:4]]
-    both = jnp.concatenate(
-        [jnp.concatenate(right, axis=0), jnp.concatenate(turned, axis=0)], axis=1
-    )
-    dims = (((0,), (0,)), ((), ()))
-    result = lax.dot_general(left, both, dims, preferred_element_type=jnp.float32)
-    result = (result * scaling).astype(jnp.bfloat16)
-    for group in range(out.shape[0]):
-        first_row = group // 8 * 256 + group // 4 % 2 * 128 + group % 2 * 64
+    columns = pl.ds(pl.multiple_of(block * width, width), width)
+
+    def multiply(left, right):
+        turned = right[4:] + [-piece for piece in right[:4]]
+        both = jnp.concatenate(
+            [jnp.concatenate(right, axis=0), jnp.concatenate(turned, axis=0)], axis=1
+        )
+        dims = (((0,), (0,)), ((), ()))
+        result = lax.dot_general(
+            jnp.concatenate(left, axis=0), both, dims, preferred_element_type=jnp.float32
+        )
+        return (result * scaling).astype(jnp.bfloat16)
+
+    def store(group, first_row, first_col, result):
+        size = result.shape[1] // 2
         for part in range(2):
-            first_col = part * width + group // 2 % 2 * 128
-            out[group, part, 0] = result[first_row : first_row + 64, first_col : first_col + 128]
-
-
-def product(y, blocks, scaling, devices):
+            for goal_core in range(2):
+                row, col = first_row + goal_core * 64, part * size + first_col
+                out[group, goal_core, part, 0] = result[row : row + 64, col : col + 128]
+
+    whole = [block[part, 0] for part in range(2) for block in blocks]
+    narrow = [block[part, 0, :, columns] for part in range(2) for block in blocks]
+
+    @pl.when(core == 0)
+    def _():
+        result = multiply(whole, narrow)
+        for group in range(16):
+            x, z_hi, z_lo = group // 4, group // 2 % 2, group % 2
+            store(group, x * 256 + z_hi * 128, z_lo * 128, result)
+
+    @pl.when(core == 1)
+    def _():
+        result = multiply(narrow, whole)
+        for group in range(16):
+            y, z_hi, z_lo = group // 4, group // 2 % 2, group % 2
+            store(group, z_hi * 128, y * 256 + z_lo * 128, result)
+
+
+def product(blocks, scaling, devices):
     _, nb, windows, stations = blocks[0].shape
     spec = pl.BlockSpec((2, 1, windows, stations), lambda i: (0, i, 0, 0))
     return pl.pallas_call(
         functools.partial(product_kernel, scaling=scaling),
         grid=(nb,),
-        in_specs=[pl.BlockSpec(memory_space=pltpu.SMEM)] + [spec] * 4,
-        out_specs=pl.BlockSpec((devices, 2, 1, 64, 128), lambda i: (0, 0, i, 0, 0)),
-        out_shape=jax.ShapeDtypeStruct((devices, 2, nb, 64, 128), jnp.bfloat16),
+        in_specs=[spec] * 4,
+        out_specs=pl.BlockSpec((devices, 2, 2, 1, 64, 128), lambda i: (0, 0, 0, i, 0, 0)),
+        out_shape=jax.ShapeDtypeStruct((devices, 2, 2, nb, 64, 128), jnp.bfloat16),
         compiler_params=pltpu.CompilerParams(vmem_limit_bytes=VMEM),
         cost_estimate=pl.CostEstimate(
             flops=nb * 2**28, bytes_accessed=nb * 2**21, transcendentals=0
         ),
         name="product",
-    )(y, *blocks)
-
-
-def place_kernel(in_ref, *refs, start, stride):
+    )(*blocks)
+
+
+def place_kernel(in_ref, *refs, start, half_bins, own):
     out, buffer, in_sems, out_sems = refs[-4:]
-    devices, _, nb = buffer.shape[:3]
+    devices, nb = in_ref.shape[0], in_ref.shape[3]
+    core, _ = own_place()
+    first = start + (core if own else 1 - core) * half_bins
     arrivals = [
-        pltpu.make_async_copy(in_ref.at[i], buffer.at[i], in_sems.at[i]) for i in range(devices)
-    ]
+        pltpu.make_async_copy(
+            in_ref.at[i, core], buffer.at[:, pl.ds(i * nb, nb)], in_sems.at[i]
+        )
+        for i in range(devices)
+    ]
+    parts = out_sems.shape[0]
+    size = devices // parts * nb
     departures = [
         pltpu.make_async_copy(
-            buffer.at[i], out.at[:, pl.ds(start + i * stride, nb)], out_sems.at[i]
-        )
-        for i in range(devices)
+            buffer.at[:, pl.ds(i * size, size)],
+            out.at[:, pl.ds(first + i * size, size)],
+            out_sems.at[i],
+        )
+        for i in range(parts)
     ]
     for arrival in arrivals:
         arrival.start()
-    for arrival, departure in zip(arrivals, departures):
-        arrival.wait()
-        departure.start()
+    for i in range(parts):
+        for arrival in arrivals[i * devices // parts : (i + 1) * devices // parts]:
+            arrival.wait()
+        departures[i].start()
     for departure in departures:
         departure.wait()
 
 
-def place_blocks(array, total, start, stride, shape):
+def place_blocks(array, total, start, shape, own):
     anywhere = pl.BlockSpec(memory_space=pl.ANY)
     operands = [array] + ([] if total is None else [total])
-    devices = array.shape[0]
+    devices, _, parts, nb, rows, cols = array.shape
     return pl.pallas_call(
-        functools.partial(place_kernel, start=start, stride=stride),
+        functools.partial(place_kernel, start=start, half_bins=shape.shape[1] // 2, own=own),
         in_specs=[anywhere] * len(operands),
         out_specs=anywhere,
         out_shape=shape,
         scratch_shapes=[
-            pltpu.VMEM(array.shape, array.dtype),
+            pltpu.VMEM((parts, devices * nb, rows, cols), array.dtype),
             pltpu.SemaphoreType.DMA((devices,)),
-            pltpu.SemaphoreType.DMA((devices,)),
+            pltpu.SemaphoreType.DMA((2,)),
         ],
         input_output_aliases={} if total is None else {1: 0},
         compiler_params=pltpu.CompilerParams(vmem_limit_bytes=VMEM),
@@ -304,23 +364,27 @@
 
 
 def body(waveform, valid_mask, band_starts, station_map):
-    y = (lax.axis_index("col") // 2).astype(jnp.int32).reshape(1)
     stations = waveform.shape[1]
     windows = waveform.shape[0] * lax.axis_size("row") * lax.axis_size("col")
     bins = BINS * band_starts.shape[0]
     scaling = float(windows) ** (-0.5)
-    devices = len(LINES[0])
-    spectra = make_spectra(
+    devices = len(PLANES[0])
+    own, other = make_spectra(
         waveform[0], valid_mask, band_starts, station_map.reshape(1, stations), devices
     )
-    woven = weave(exchange(spectra), stations)
+    spectra = exchange(jnp.stack([own, swap(other)], axis=1))
+    woven = weave(spectra.reshape(2 * devices, *own.shape[1:]), stations)
     shape = jax.ShapeDtypeStruct((2, bins, 64, 128), jnp.bfloat16)
     total = None
     start = 0
     for part in woven:
-        blocks = exchange(product(y, gather(part), scaling, devices))
-        total = place_blocks(blocks, total, start, sum(PARTS), shape)
-        start += part.shape[1]
+        blocks = exchange(product(gather(part), scaling, devices))
+        if total is not None:
+            total, blocks = lax.optimization_barrier((total, blocks))
+        given = swap(blocks)
+        total = place_blocks(blocks, total, start, shape, True)
+        total = place_blocks(given, total, start, shape, False)
+        start += part.shape[1] * devices
     return total
 
 

time: 147 us -> 141 us (0.959)
  the two profiles are of different devices: /device:TPU:1 before, /device:TPU:15 now
where the time goes in v3:
time: 141 us; the launch traced here: 139 us
  waiting for transfers between devices  65.1 us (46%)
  Pallas kernels  35 us (25%)
  starting transfers between devices  18.9 us (13%)
  blocking collectives  17.6 us (12%)
    ppermute x9, waiting for transfers between devices, permute(): return lax.ppermute(array, AXES, pairs)  34.9 us
    all_to_all x2, waiting for transfers between devices, exchange(): lax.all_to_all(array, AXES, 0, 0, axis_index_groups=PLANES, tiled=True)  30.2 us
    all_to_all x1, blocking collectives, exchange(): lax.all_to_all(array, AXES, 0, 0, axis_index_groups=PLANES, tiled=True)  17.6 us
    pallas_call x1, Pallas kernels, make_spectra(): pl.pallas_call(functools.partial(spectra_kernel, length=length, band_coun...  15.4 us
    all_to_all x2, starting transfers between devices, exchange(): lax.all_to_all(array, AXES, 0, 0, axis_index_groups=PLANES, tiled=True)  12.6 us
    pallas_call x4, Pallas kernels, place_blocks(): pl.pallas_call(functools.partial(place_kernel, start=start, half_bins=sha...  9.38 us
    pallas_call x2, Pallas kernels, product(): pl.pallas_call(functools.partial(product_kernel, scaling=scaling), grid=(...  7.93 us
    ppermute x9, starting transfers between devices, permute(): return lax.ppermute(array, AXES, pairs)  6.2 us
  transfers between devices with their start and end apart: 11, of which 10 were waited for; matrix products, arithmetic and copies ran while one was open for 0% of the time, Pallas kernels for 8%

profile of v3, /device:TPU:15, one launch (start us, length us, event | category | flops | bytes accessed | tf_op | source)
XLA Modules:
  0.0 138.5 jit_solution(13962916668559872065)
XLA Ops:
  0.0 15.4 %spectra.1 = (bf16[16,80,128]{2,1,0:T(8,128)(2,1)}, bf16[16,80,128]{2,1,0:T(8,128)(2,1)}) custom-call(s32[10]{0:T(128)} %band_ref.1, bf16[1024,8192]{1,0:T(8,128)(2,1)} %bitcast.8, s32[1,1024]{1,0:T(1,128)} %mask_ref.1, s32[1,1024]{1,0:T(1,128)} %bitcast.9, bf16[2,320,320]{2,1,0:T(8,128)(2,1)} %constant.2.clone.order_ref), custom_call_target="tpu_custom_call" | custom-call | flops 5368709120 | bytes 16777216 | tf_op jit(solution)/shard_map/spectra/pallas_call | solution.py:202
  16.2 1.5 %collective-permute-done = bf16[16,80,128]{2,1,0:T(8,128)(2,1)S(1)} collective-permute-done((bf16[16,80,128]{2,1,0:T(8,128)(2,1)}, bf16[16,80,128]{2,1,0:T(8,128)(2,1)S(1)}, u32[]{:S(2)}, u32[]{:S(2)}) %collective-permute-start) | collective-permute-done | bytes 327712 | tf_op jit(solution)/shard_map/ppermute | solution.py:46
  18.7 17.6 %all_to_all.15 = bf16[16,2,80,128]{3,2,1,0:T(8,128)(2,1)} all-to-all(bf16[16,2,80,128]{3,2,1,0:T(8,128)(2,1)S(1)} %copy.10), channel_id=1, replica_groups={{0,1,16,17,32,33,48,49,64,65,80,81,96,97,112,113},{2,3,18,19,34,35,50,5..., dimensions={0} | all-to-all | bytes 1310720 | tf_op jit(solution)/shard_map/all_to_all | solution.py:38
  36.3 2.3 %weave.1 = (bf16[2,2,32,1024]{3,2,1,0:T(8,128)(2,1)}, bf16[2,3,32,1024]{3,2,1,0:T(8,128)(2,1)}) custom-call(bf16[32,80,128]{2,1,0:T(8,128)(2,1)} %bitcast.5), custom_call_target="tpu_custom_call" | custom-call | tf_op jit(solution)/shard_map/weave/pallas_call | solution.py:246
  38.6 2.4 %collective-permute-start.2 = (bf16[2,2,32,1024]{3,2,1,0:T(8,128)(2,1)}, bf16[2,2,32,1024]{3,2,1,0:T(8,128)(2,1)S(1)}, u32[]{:S(2)}, u32[]{:S(2)}) collective-permute-start(bf16[2,2,32,1024]{3,2,1,0:T(8,128)(2,1)} %get-tuple-element.13.refs_0_), channel_id=1, source_target_pairs={{0,4},{8,72},{1,5},{9,73},{16,20},{24,88},{17,21},{25,89},{2,6},{1... | collective-permute-start | bytes 786440 | tf_op jit(solution)/shard_map/ppermute | solution.py:46
  41.0 3.4 %collective-permute-done.1.refs_1_ = bf16[2,2,32,1024]{3,2,1,0:T(8,128)(2,1)S(1)} collective-permute-done((bf16[2,2,32,1024]{3,2,1,0:T(8,128)(2,1)}, bf16[2,2,32,1024]{3,2,1,0:T(8,128)(2,1)S(1)}, u32[]{:S(2)}, u32[]{:S(2)}) %collective-permute-start.1) | collective-permute-done | bytes 262176 | tf_op jit(solution)/shard_map/ppermute | solution.py:46
  44.4 1.3 collective-permute-done.2.refs_2_
  45.6 2.9 %collective-permute-done.3.refs_3_ = bf16[2,2,32,1024]{3,2,1,0:T(8,128)(2,1)} collective-permute-done((bf16[2,2,32,1024]{3,2,1,0:T(8,128)(2,1)}, bf16[2,2,32,1024]{3,2,1,0:T(8,128)(2,1)}, u32[]{:S(2)}, u32[]{:S(2)}) %collective-permute-start.3) | collective-permute-done | bytes 262176 | tf_op jit(solution)/shard_map/ppermute | solution.py:46
  48.5 3.1 %product.2 = bf16[16,2,2,2,64,128]{5,4,3,2,1,0:T(8,128)(2,1)} custom-call(bf16[2,2,32,1024]{3,2,1,0:T(8,128)(2,1)} %get-tuple-element.13.refs_0_, bf16[2,2,32,1024]{3,2,1,0:T(8,128)(2,1)} %copy-done.3, bf16[2,2,32,1024]{3,2,1,0:T(8,128)(2,1)} %copy-done.4, bf16[2,2,32,1024]{3,2,1,0:T(8,128)(2,1)} %collective-permute-done.3.refs_3_), custom_call_target="tpu_custom_call" | custom-call | flops 536870912 | bytes 4194304 | tf_op jit(solution)/shard_map/product/pallas_call | solution.py:301
  51.7 5.7 %all-to-all-start.1 = ((bf16[16,2,2,2,64,128]{5,4,3,2,1,0:T(8,128)(2,1)}), bf16[16,2,2,2,64,128]{5,4,3,2,1,0:T(8,128)(2,1)}, u32[]{:S(2)}, u32[]{:S(2)}) async-start(bf16[16,2,2,2,64,128]{5,4,3,2,1,0:T(8,128)(2,1)} %product.2), calls=%async_computation.1 | async-start | bytes 4194304 | tf_op jit(solution)/shard_map/all_to_all | solution.py:38
  57.4 1.2 collective-permute-start.5
  58.6 1.5 %collective-permute-start.6 = (bf16[2,3,32,1024]{3,2,1,0:T(8,128)(2,1)S(1)}, bf16[2,3,32,1024]{3,2,1,0:T(8,128)(2,1)S(1)}, u32[]{:S(2)}, u32[]{:S(2)}) collective-permute-start(bf16[2,3,32,1024]{3,2,1,0:T(8,128)(2,1)S(1)} %copy-done), channel_id=1, source_target_pairs={{0,4},{8,72},{1,5},{9,73},{16,20},{24,88},{17,21},{25,89},{2,6},{1... | collective-permute-start | bytes 1179656 | tf_op jit(solution)/shard_map/ppermute | solution.py:46
  60.1 5.4 %collective-permute-done.5.refs_1_ = bf16[2,3,32,1024]{3,2,1,0:T(8,128)(2,1)S(1)} collective-permute-done((bf16[2,3,32,1024]{3,2,1,0:T(8,128)(2,1)S(1)}, bf16[2,3,32,1024]{3,2,1,0:T(8,128)(2,1)S(1)}, u32[]{:S(2)}, u32[]{:S(2)}) %collective-permute-start.5) | collective-permute-done | bytes 393248 | tf_op jit(solution)/shard_map/ppermute | solution.py:46
  65.5 4.9 %collective-permute-done.6.refs_2_ = bf16[2,3,32,1024]{3,2,1,0:T(8,128)(2,1)S(1)} collective-permute-done((bf16[2,3,32,1024]{3,2,1,0:T(8,128)(2,1)S(1)}, bf16[2,3,32,1024]{3,2,1,0:T(8,128)(2,1)S(1)}, u32[]{:S(2)}, u32[]{:S(2)}) %collective-permute-start.6) | collective-permute-done | bytes 393248 | tf_op jit(solution)/shard_map/ppermute | solution.py:46
  71.2 10.2 %collective-permute-done.7.refs_3_ = bf16[2,3,32,1024]{3,2,1,0:T(8,128)(2,1)} collective-permute-done((bf16[2,3,32,1024]{3,2,1,0:T(8,128)(2,1)S(1)}, bf16[2,3,32,1024]{3,2,1,0:T(8,128)(2,1)}, u32[]{:S(2)}, u32[]{:S(2)}) %collective-permute-start.7) | collective-permute-done | bytes 393248 | tf_op jit(solution)/shard_map/ppermute | solution.py:46
  81.4 4.8 %product.3 = bf16[16,2,2,3,64,128]{5,4,3,2,1,0:T(8,128)(2,1)} custom-call(bf16[2,3,32,1024]{3,2,1,0:T(8,128)(2,1)} %get-tuple-element.14.refs_0_, bf16[2,3,32,1024]{3,2,1,0:T(8,128)(2,1)} %copy-done.1, bf16[2,3,32,1024]{3,2,1,0:T(8,128)(2,1)} %copy-done.2, bf16[2,3,32,1024]{3,2,1,0:T(8,128)(2,1)} %collective-permute-done.7.refs_3_), custom_call_target="tpu_custom_call" | custom-call | flops 805306368 | bytes 6291456 | tf_op jit(solution)/shard_map/product/pallas_call | solution.py:301
  86.2 6.9 %all-to-all-start.2 = ((bf16[16,2,2,3,64,128]{5,4,3,2,1,0:T(8,128)(2,1)}), bf16[16,2,2,3,64,128]{5,4,3,2,1,0:T(8,128)(2,1)}, u32[]{:S(2)}, u32[]{:S(2)}) async-start(bf16[16,2,2,3,64,128]{5,4,3,2,1,0:T(8,128)(2,1)} %product.3), calls=%async_computation.2 | async-start | bytes 6291456 | tf_op jit(solution)/shard_map/all_to_all | solution.py:38
  93.1 2.2 %place.4.refs_0_ = bf16[2,160,64,128]{3,2,1,0:T(8,128)(2,1)} custom-call(bf16[16,2,2,2,64,128]{5,4,3,2,1,0:T(8,128)(2,1)} %all-to-all-done.1.in_ref), custom_call_target="tpu_custom_call" | custom-call | tf_op jit(solution)/shard_map/place/pallas_call | solution.py:350
  95.3 2.3 %collective-permute-done.4.in_ref = bf16[16,2,2,2,64,128]{5,4,3,2,1,0:T(8,128)(2,1)} collective-permute-done((bf16[16,2,2,2,64,128]{5,4,3,2,1,0:T(8,128)(2,1)}, bf16[16,2,2,2,64,128]{5,4,3,2,1,0:T(8,128)(2,1)}, u32[]{:S(2)}, u32[]{:S(2)}) %collective-permute-start.4) | collective-permute-done | bytes 2097184 | tf_op jit(solution)/shard_map/ppermute | solution.py:46
  97.6 2.2 %place.5.refs_0_ = bf16[2,160,64,128]{3,2,1,0:T(8,128)(2,1)} custom-call(bf16[16,2,2,2,64,128]{5,4,3,2,1,0:T(8,128)(2,1)} %collective-permute-done.4.in_ref, bf16[2,160,64,128]{3,2,1,0:T(8,128)(2,1)} %place.4.refs_0_), custom_call_target="tpu_custom_call", output_to_operand_aliasing={{}: (1, {})} | custom-call | tf_op jit(solution)/shard_map/place/pallas_call | solution.py:350
  99.8 30.2 %all-to-all-done.2.in_ref = bf16[16,2,2,3,64,128]{5,4,3,2,1,0:T(8,128)(2,1)} async-done(((bf16[16,2,2,3,64,128]{5,4,3,2,1,0:T(8,128)(2,1)}), bf16[16,2,2,3,64,128]{5,4,3,2,1,0:T(8,128)(2,1)}, u32[]{:S(2)}, u32[]{:S(2)}) %all-to-all-start.2) | async-done | bytes 3145760 | tf_op jit(solution)/shard_map/all_to_all | solution.py:38
  130.4 2.5 %place.6.refs_0_ = bf16[2,160,64,128]{3,2,1,0:T(8,128)(2,1)} custom-call(bf16[16,2,2,3,64,128]{5,4,3,2,1,0:T(8,128)(2,1)} %all-to-all-done.2.in_ref, bf16[2,160,64,128]{3,2,1,0:T(8,128)(2,1)} %place.5.refs_0_), custom_call_target="tpu_custom_call", output_to_operand_aliasing={{}: (1, {})} | custom-call | tf_op jit(solution)/shard_map/place/pallas_call | solution.py:350
  132.9 3.1 %collective-permute-done.8.in_ref = bf16[16,2,2,3,64,128]{5,4,3,2,1,0:T(8,128)(2,1)} collective-permute-done((bf16[16,2,2,3,64,128]{5,4,3,2,1,0:T(8,128)(2,1)}, bf16[16,2,2,3,64,128]{5,4,3,2,1,0:T(8,128)(2,1)}, u32[]{:S(2)}, u32[]{:S(2)}) %collective-permute-start.8) | collective-permute-done | bytes 3145760 | tf_op jit(solution)/shard_map/ppermute | solution.py:46
  136.0 2.5 %place.7 = bf16[2,160,64,128]{3,2,1,0:T(8,128)(2,1)} custom-call(bf16[16,2,2,3,64,128]{5,4,3,2,1,0:T(8,128)(2,1)} %collective-permute-done.8.in_ref, bf16[2,160,64,128]{3,2,1,0:T(8,128)(2,1)} %place.6.refs_0_), custom_call_target="tpu_custom_call", output_to_operand_aliasing={{}: (1, {})} | custom-call | tf_op jit(solution)/shard_map/place/pallas_call | solution.py:350
  (19 shorter events, 3.0 us)
Async XLA Ops:
  15.4 2.2 %collective-permute-start = (bf16[16,80,128]{2,1,0:T(8,128)(2,1)}, bf16[16,80,128]{2,1,0:T(8,128)(2,1)S(1)}, u32[]{:S(2)}, u32[]{:S(2)}) collective-permute-start(bf16[16,80,128]{2,1,0:T(8,128)(2,1)} %get-tuple-element.12), channel_id=1, source_target_pairs={{0,8},{8,0},{1,9},{9,1},{16,24},{24,16},{17,25},{25,17},{2,10},{10... | collective-permute-start | bytes 983048 | tf_op jit(solution)/shard_map/ppermute | solution.py:46
  38.6 18.7 %copy-start = (bf16[2,3,32,1024]{3,2,1,0:T(8,128)(2,1)S(1)}, bf16[2,3,32,1024]{3,2,1,0:T(8,128)(2,1)}, u32[]{:S(2)}) copy-start(bf16[2,3,32,1024]{3,2,1,0:T(8,128)(2,1)} %get-tuple-element.14.refs_0_) | copy-start | bytes 1179652
  38.6 5.7 %collective-permute-start.1 = (bf16[2,2,32,1024]{3,2,1,0:T(8,128)(2,1)}, bf16[2,2,32,1024]{3,2,1,0:T(8,128)(2,1)S(1)}, u32[]{:S(2)}, u32[]{:S(2)}) collective-permute-start(bf16[2,2,32,1024]{3,2,1,0:T(8,128)(2,1)} %get-tuple-element.13.refs_0_), channel_id=1, source_target_pairs={{0,2},{8,40},{1,3},{9,41},{16,18},{24,56},{17,19},{25,57},{2,4},{1... | collective-permute-start | bytes 786440 | tf_op jit(solution)/shard_map/ppermute | solution.py:46
  38.6 7.0 %collective-permute-start.2 = (bf16[2,2,32,1024]{3,2,1,0:T(8,128)(2,1)}, bf16[2,2,32,1024]{3,2,1,0:T(8,128)(2,1)S(1)}, u32[]{:S(2)}, u32[]{:S(2)}) collective-permute-start(bf16[2,2,32,1024]{3,2,1,0:T(8,128)(2,1)} %get-tuple-element.13.refs_0_), channel_id=1, source_target_pairs={{0,4},{8,72},{1,5},{9,73},{16,20},{24,88},{17,21},{25,89},{2,6},{1... | collective-permute-start | bytes 786440 | tf_op jit(solution)/shard_map/ppermute | solution.py:46
  41.0 7.5 %collective-permute-start.3 = (bf16[2,2,32,1024]{3,2,1,0:T(8,128)(2,1)}, bf16[2,2,32,1024]{3,2,1,0:T(8,128)(2,1)}, u32[]{:S(2)}, u32[]{:S(2)}) collective-permute-start(bf16[2,2,32,1024]{3,2,1,0:T(8,128)(2,1)} %get-tuple-element.13.refs_0_), channel_id=1, source_target_pairs={{0,6},{8,104},{1,7},{9,105},{16,22},{24,120},{17,23},{25,121},{2,0... | collective-permute-start | bytes 786440 | tf_op jit(solution)/shard_map/ppermute | solution.py:46
  44.4 4.2 %copy-start.3 = (bf16[2,2,32,1024]{3,2,1,0:T(8,128)(2,1)}, bf16[2,2,32,1024]{3,2,1,0:T(8,128)(2,1)S(1)}, u32[]{:S(2)}) copy-start(bf16[2,2,32,1024]{3,2,1,0:T(8,128)(2,1)S(1)} %collective-permute-done.1.refs_1_) | copy-start | bytes 786436
  45.6 2.9 %copy-start.4 = (bf16[2,2,32,1024]{3,2,1,0:T(8,128)(2,1)}, bf16[2,2,32,1024]{3,2,1,0:T(8,128)(2,1)S(1)}, u32[]{:S(2)}) copy-start(bf16[2,2,32,1024]{3,2,1,0:T(8,128)(2,1)S(1)} %collective-permute-done.2.refs_2_) | copy-start | bytes 786436
  51.7 34.5 %all-to-all-start.1 = ((bf16[16,2,2,2,64,128]{5,4,3,2,1,0:T(8,128)(2,1)}), bf16[16,2,2,2,64,128]{5,4,3,2,1,0:T(8,128)(2,1)}, u32[]{:S(2)}, u32[]{:S(2)}) async-start(bf16[16,2,2,2,64,128]{5,4,3,2,1,0:T(8,128)(2,1)} %product.2), calls=%async_computation.1 | async-start | bytes 4194304 | tf_op jit(solution)/shard_map/all_to_all | solution.py:38
  57.4 8.1 %collective-permute-start.5 = (bf16[2,3,32,1024]{3,2,1,0:T(8,128)(2,1)S(1)}, bf16[2,3,32,1024]{3,2,1,0:T(8,128)(2,1)S(1)}, u32[]{:S(2)}, u32[]{:S(2)}) collective-permute-start(bf16[2,3,32,1024]{3,2,1,0:T(8,128)(2,1)S(1)} %copy-done), channel_id=1, source_target_pairs={{0,2},{8,40},{1,3},{9,41},{16,18},{24,56},{17,19},{25,57},{2,4},{1... | collective-permute-start | bytes 1179656 | tf_op jit(solution)/shard_map/ppermute | solution.py:46
  58.6 11.8 %collective-permute-start.6 = (bf16[2,3,32,1024]{3,2,1,0:T(8,128)(2,1)S(1)}, bf16[2,3,32,1024]{3,2,1,0:T(8,128)(2,1)S(1)}, u32[]{:S(2)}, u32[]{:S(2)}) collective-permute-start(bf16[2,3,32,1024]{3,2,1,0:T(8,128)(2,1)S(1)} %copy-done), channel_id=1, source_target_pairs={{0,4},{8,72},{1,5},{9,73},{16,20},{24,88},{17,21},{25,89},{2,6},{1... | collective-permute-start | bytes 1179656 | tf_op jit(solution)/shard_map/ppermute | solution.py:46
  60.1 21.3 %collective-permute-start.7 = (bf16[2,3,32,1024]{3,2,1,0:T(8,128)(2,1)S(1)}, bf16[2,3,32,1024]{3,2,1,0:T(8,128)(2,1)}, u32[]{:S(2)}, u32[]{:S(2)}) collective-permute-start(bf16[2,3,32,1024]{3,2,1,0:T(8,128)(2,1)S(1)} %copy-done), channel_id=1, source_target_pairs={{0,6},{8,104},{1,7},{9,105},{16,22},{24,120},{17,23},{25,121},{2,0... | collective-permute-start | bytes 1179656 | tf_op jit(solution)/shard_map/ppermute | solution.py:46
  65.5 15.8 %copy-start.1 = (bf16[2,3,32,1024]{3,2,1,0:T(8,128)(2,1)}, bf16[2,3,32,1024]{3,2,1,0:T(8,128)(2,1)S(1)}, u32[]{:S(2)}) copy-start(bf16[2,3,32,1024]{3,2,1,0:T(8,128)(2,1)S(1)} %collective-permute-done.5.refs_1_) | copy-start | bytes 1179652
  70.4 0.7 copy-start.2
  86.2 43.9 %all-to-all-start.2 = ((bf16[16,2,2,3,64,128]{5,4,3,2,1,0:T(8,128)(2,1)}), bf16[16,2,2,3,64,128]{5,4,3,2,1,0:T(8,128)(2,1)}, u32[]{:S(2)}, u32[]{:S(2)}) async-start(bf16[16,2,2,3,64,128]{5,4,3,2,1,0:T(8,128)(2,1)} %product.3), calls=%async_computation.2 | async-start | bytes 6291456 | tf_op jit(solution)/shard_map/all_to_all | solution.py:38
  93.1 4.5 %collective-permute-start.4 = (bf16[16,2,2,2,64,128]{5,4,3,2,1,0:T(8,128)(2,1)}, bf16[16,2,2,2,64,128]{5,4,3,2,1,0:T(8,128)(2,1)}, u32[]{:S(2)}, u32[]{:S(2)}) collective-permute-start(bf16[16,2,2,2,64,128]{5,4,3,2,1,0:T(8,128)(2,1)} %all-to-all-done.1.in_ref), channel_id=1, source_target_pairs={{0,8},{8,0},{1,9},{9,1},{16,24},{24,16},{17,25},{25,17},{2,10},{10... | collective-permute-start | bytes 6291464 | tf_op jit(solution)/shard_map/ppermute | solution.py:46
  130.0 6.0 %collective-permute-start.8 = (bf16[16,2,2,3,64,128]{5,4,3,2,1,0:T(8,128)(2,1)}, bf16[16,2,2,3,64,128]{5,4,3,2,1,0:T(8,128)(2,1)}, u32[]{:S(2)}, u32[]{:S(2)}) collective-permute-start(bf16[16,2,2,3,64,128]{5,4,3,2,1,0:T(8,128)(2,1)} %all-to-all-done.2.in_ref), channel_id=1, source_target_pairs={{0,8},{8,0},{1,9},{9,1},{16,24},{24,16},{17,25},{25,17},{2,10},{10... | collective-permute-start | bytes 9437192 | tf_op jit(solution)/shard_map/ppermute | solution.py:46

commit v4 on v3

--- a/solution.py
+++ b/solution.py
@@ -254,7 +254,8 @@
 
 
 def product_kernel(*refs, scaling):
-    blocks, out = refs[:4], refs[4]
+    blocks, goal, out, sems = refs[:4], refs[4], refs[5], refs[6]
+    copies = []
     core, block = own_place()
     width = 256
     columns = pl.ds(pl.multiple_of(block * width, width), width)
@@ -270,39 +271,51 @@
         )
         return (result * scaling).astype(jnp.bfloat16)
 
-    def store(group, first_row, first_col, result):
+    def store(group, j, first_row, first_col, result):
         size = result.shape[1] // 2
         for part in range(2):
             for goal_core in range(2):
                 row, col = first_row + goal_core * 64, part * size + first_col
-                out[group, goal_core, part, 0] = result[row : row + 64, col : col + 128]
-
-    whole = [block[part, 0] for part in range(2) for block in blocks]
-    narrow = [block[part, 0, :, columns] for part in range(2) for block in blocks]
-
-    @pl.when(core == 0)
-    def _():
-        result = multiply(whole, narrow)
-        for group in range(16):
-            x, z_hi, z_lo = group // 4, group // 2 % 2, group % 2
-            store(group, x * 256 + z_hi * 128, z_lo * 128, result)
-
-    @pl.when(core == 1)
-    def _():
-        result = multiply(narrow, whole)
-        for group in range(16):
-            y, z_hi, z_lo = group // 4, group // 2 % 2, group % 2
-            store(group, z_hi * 128, y * 256 + z_lo * 128, result)
+                out[group, goal_core, part, j] = result[row : row + 64, col : col + 128]
+
+    for j in range(out.shape[3]):
+        whole = [block[part, j] for part in range(2) for block in blocks]
+        narrow = [block[part, j, :, columns] for part in range(2) for block in blocks]
+
+        @pl.when(core == 0)
+        def _(j=j, whole=whole, narrow=narrow):
+            result = multiply(whole, narrow)
+            for group in range(16):
+                x, z_hi, z_lo = group // 4, group // 2 % 2, group % 2
+                store(group, j, x * 256 + z_hi * 128, z_lo * 128, result)
+
+        @pl.when(core == 1)
+        def _(j=j, whole=whole, narrow=narrow):
+            result = multiply(narrow, whole)
+            for group in range(16):
+                y, z_hi, z_lo = group // 4, group // 2 % 2, group % 2
+                store(group, j, z_hi * 128, y * 256 + z_lo * 128, result)
+
+        copies.append(
+            pltpu.make_async_copy(out.at[:, :, :, j], goal.at[:, :, :, j], sems.at[j])
+        )
+        copies[j].start()
+    for copy in copies:
+        copy.wait()
 
 
 def product(blocks, scaling, devices):
     _, nb, windows, stations = blocks[0].shape
-    spec = pl.BlockSpec((2, 1, windows, stations), lambda i: (0, i, 0, 0))
+    spec = pl.BlockSpec((2, nb, windows, stations), lambda i: (0, 0, 0, 0))
     return pl.pallas_call(
         functools.partial(product_kernel, scaling=scaling),
-        grid=(nb,),
+        grid=(1,),
         in_specs=[spec] * 4,
-        out_specs=pl.BlockSpec((devices, 2, 2, 1, 64, 128), lambda i: (0, 0, 0, i, 0, 0)),
+        out_specs=pl.BlockSpec(memory_space=pl.ANY),
+        scratch_shapes=[
+            pltpu.VMEM((devices, 2, 2, nb, 64, 128), jnp.bfloat16),
+            pltpu.SemaphoreType.DMA((nb,)),
+        ],
         out_shape=jax.ShapeDtypeStruct((devices, 2, 2, nb, 64, 128), jnp.bfloat16),
         compiler_params=pltpu.CompilerParams(vmem_limit_bytes=VMEM),
         cost_estimate=pl.CostEstimate(
@@ -355,7 +368,7 @@
         scratch_shapes=[
             pltpu.VMEM((parts, devices * nb, rows, cols), array.dtype),
             pltpu.SemaphoreType.DMA((devices,)),
-            pltpu.SemaphoreType.DMA((2,)),
+            pltpu.SemaphoreType.DMA((4,)),
         ],
         input_output_aliases={} if total is None else {1: 0},
         compiler_params=pltpu.CompilerParams(vmem_limit_bytes=VMEM),

time: 141 us -> 140 us (level)
  no operation moved by 1% of the time
where the time goes in v4:
time: 140 us; the launch traced here: 138 us
  waiting for transfers between devices  65.4 us (47%)
  Pallas kernels  34 us (24%)
  starting transfers between devices  18.9 us (13%)
  blocking collectives  17.6 us (13%)
    ppermute x9, waiting for transfers between devices, permute(): return lax.ppermute(array, AXES, pairs)  35.1 us
    all_to_all x2, waiting for transfers between devices, exchange(): lax.all_to_all(array, AXES, 0, 0, axis_index_groups=PLANES, tiled=True)  30.3 us
    all_to_all x1, blocking collectives, exchange(): lax.all_to_all(array, AXES, 0, 0, axis_index_groups=PLANES, tiled=True)  17.6 us
    pallas_call x1, Pallas kernels, make_spectra(): pl.pallas_call(functools.partial(spectra_kernel, length=length, band_coun...  15.4 us
    all_to_all x2, starting transfers between devices, exchange(): lax.all_to_all(array, AXES, 0, 0, axis_index_groups=PLANES, tiled=True)  12.7 us
    pallas_call x4, Pallas kernels, place_blocks(): pl.pallas_call(functools.partial(place_kernel, start=start, half_bins=sha...  9.02 us
    pallas_call x2, Pallas kernels, product(): pl.pallas_call(functools.partial(product_kernel, scaling=scaling), grid=(...  7.3 us
    ppermute x9, starting transfers between devices, permute(): return lax.ppermute(array, AXES, pairs)  6.24 us
  transfers between devices with their start and end apart: 11, of which 10 were waited for; matrix products, arithmetic and copies ran while one was open for 0% of the time, Pallas kernels for 8%

profile of v4, /device:TPU:15, one launch (start us, length us, event | category | flops | bytes accessed | tf_op | source)
XLA Modules:
  0.0 138.0 jit_solution(6234011467054852307)
XLA Ops:
  0.0 15.4 %spectra.1 = (bf16[16,80,128]{2,1,0:T(8,128)(2,1)}, bf16[16,80,128]{2,1,0:T(8,128)(2,1)}) custom-call(s32[10]{0:T(128)} %band_ref.1, bf16[1024,8192]{1,0:T(8,128)(2,1)} %bitcast.8, s32[1,1024]{1,0:T(1,128)} %mask_ref.1, s32[1,1024]{1,0:T(1,128)} %bitcast.9, bf16[2,320,320]{2,1,0:T(8,128)(2,1)} %constant.2.clone.order_ref), custom_call_target="tpu_custom_call" | custom-call | flops 5368709120 | bytes 16777216 | tf_op jit(solution)/shard_map/spectra/pallas_call | solution.py:202
  16.2 1.5 %collective-permute-done = bf16[16,80,128]{2,1,0:T(8,128)(2,1)S(1)} collective-permute-done((bf16[16,80,128]{2,1,0:T(8,128)(2,1)}, bf16[16,80,128]{2,1,0:T(8,128)(2,1)S(1)}, u32[]{:S(2)}, u32[]{:S(2)}) %collective-permute-start) | collective-permute-done | bytes 327712 | tf_op jit(solution)/shard_map/ppermute | solution.py:46
  18.7 17.6 %all_to_all.15 = bf16[16,2,80,128]{3,2,1,0:T(8,128)(2,1)} all-to-all(bf16[16,2,80,128]{3,2,1,0:T(8,128)(2,1)S(1)} %copy.10), channel_id=1, replica_groups={{0,1,16,17,32,33,48,49,64,65,80,81,96,97,112,113},{2,3,18,19,34,35,50,5..., dimensions={0} | all-to-all | bytes 1310720 | tf_op jit(solution)/shard_map/all_to_all | solution.py:38
  36.3 2.3 %weave.1 = (bf16[2,2,32,1024]{3,2,1,0:T(8,128)(2,1)}, bf16[2,3,32,1024]{3,2,1,0:T(8,128)(2,1)}) custom-call(bf16[32,80,128]{2,1,0:T(8,128)(2,1)} %bitcast.5), custom_call_target="tpu_custom_call" | custom-call | tf_op jit(solution)/shard_map/weave/pallas_call | solution.py:246
  38.6 2.4 %collective-permute-start.2 = (bf16[2,2,32,1024]{3,2,1,0:T(8,128)(2,1)}, bf16[2,2,32,1024]{3,2,1,0:T(8,128)(2,1)S(1)}, u32[]{:S(2)}, u32[]{:S(2)}) collective-permute-start(bf16[2,2,32,1024]{3,2,1,0:T(8,128)(2,1)} %get-tuple-element.13.refs_0_), channel_id=1, source_target_pairs={{0,4},{8,72},{1,5},{9,73},{16,20},{24,88},{17,21},{25,89},{2,6},{1... | collective-permute-start | bytes 786440 | tf_op jit(solution)/shard_map/ppermute | solution.py:46
  41.0 3.3 %collective-permute-done.1.refs_1_ = bf16[2,2,32,1024]{3,2,1,0:T(8,128)(2,1)S(1)} collective-permute-done((bf16[2,2,32,1024]{3,2,1,0:T(8,128)(2,1)}, bf16[2,2,32,1024]{3,2,1,0:T(8,128)(2,1)S(1)}, u32[]{:S(2)}, u32[]{:S(2)}) %collective-permute-start.1) | collective-permute-done | bytes 262176 | tf_op jit(solution)/shard_map/ppermute | solution.py:46
  44.4 1.3 collective-permute-done.2.refs_2_
  45.7 2.9 %collective-permute-done.3.refs_3_ = bf16[2,2,32,1024]{3,2,1,0:T(8,128)(2,1)} collective-permute-done((bf16[2,2,32,1024]{3,2,1,0:T(8,128)(2,1)}, bf16[2,2,32,1024]{3,2,1,0:T(8,128)(2,1)}, u32[]{:S(2)}, u32[]{:S(2)}) %collective-permute-start.3) | collective-permute-done | bytes 262176 | tf_op jit(solution)/shard_map/ppermute | solution.py:46
  48.5 3.2 %product.2 = bf16[16,2,2,2,64,128]{5,4,3,2,1,0:T(8,128)(2,1)} custom-call(bf16[2,2,32,1024]{3,2,1,0:T(8,128)(2,1)} %get-tuple-element.13.refs_0_, bf16[2,2,32,1024]{3,2,1,0:T(8,128)(2,1)} %copy-done.3, bf16[2,2,32,1024]{3,2,1,0:T(8,128)(2,1)} %copy-done.4, bf16[2,2,32,1024]{3,2,1,0:T(8,128)(2,1)} %collective-permute-done.3.refs_3_), custom_call_target="tpu_custom_call" | custom-call | flops 536870912 | bytes 4194304 | tf_op jit(solution)/shard_map/product/pallas_call | solution.py:310
  51.7 5.7 %all-to-all-start.1 = ((bf16[16,2,2,2,64,128]{5,4,3,2,1,0:T(8,128)(2,1)}), bf16[16,2,2,2,64,128]{5,4,3,2,1,0:T(8,128)(2,1)}, u32[]{:S(2)}, u32[]{:S(2)}) async-start(bf16[16,2,2,2,64,128]{5,4,3,2,1,0:T(8,128)(2,1)} %product.2), calls=%async_computation.1 | async-start | bytes 4194304 | tf_op jit(solution)/shard_map/all_to_all | solution.py:38
  57.5 1.3 collective-permute-start.5
  58.7 1.5 %collective-permute-start.6 = (bf16[2,3,32,1024]{3,2,1,0:T(8,128)(2,1)S(1)}, bf16[2,3,32,1024]{3,2,1,0:T(8,128)(2,1)S(1)}, u32[]{:S(2)}, u32[]{:S(2)}) collective-permute-start(bf16[2,3,32,1024]{3,2,1,0:T(8,128)(2,1)S(1)} %copy-done), channel_id=1, source_target_pairs={{0,4},{8,72},{1,5},{9,73},{16,20},{24,88},{17,21},{25,89},{2,6},{1... | collective-permute-start | bytes 1179656 | tf_op jit(solution)/shard_map/ppermute | solution.py:46
  60.2 5.4 %collective-permute-done.5.refs_1_ = bf16[2,3,32,1024]{3,2,1,0:T(8,128)(2,1)S(1)} collective-permute-done((bf16[2,3,32,1024]{3,2,1,0:T(8,128)(2,1)S(1)}, bf16[2,3,32,1024]{3,2,1,0:T(8,128)(2,1)S(1)}, u32[]{:S(2)}, u32[]{:S(2)}) %collective-permute-start.5) | collective-permute-done | bytes 393248 | tf_op jit(solution)/shard_map/ppermute | solution.py:46
  65.6 5.0 %collective-permute-done.6.refs_2_ = bf16[2,3,32,1024]{3,2,1,0:T(8,128)(2,1)S(1)} collective-permute-done((bf16[2,3,32,1024]{3,2,1,0:T(8,128)(2,1)S(1)}, bf16[2,3,32,1024]{3,2,1,0:T(8,128)(2,1)S(1)}, u32[]{:S(2)}, u32[]{:S(2)}) %collective-permute-start.6) | collective-permute-done | bytes 393248 | tf_op jit(solution)/shard_map/ppermute | solution.py:46
  71.3 10.2 %collective-permute-done.7.refs_3_ = bf16[2,3,32,1024]{3,2,1,0:T(8,128)(2,1)} collective-permute-done((bf16[2,3,32,1024]{3,2,1,0:T(8,128)(2,1)S(1)}, bf16[2,3,32,1024]{3,2,1,0:T(8,128)(2,1)}, u32[]{:S(2)}, u32[]{:S(2)}) %collective-permute-start.7) | collective-permute-done | bytes 393248 | tf_op jit(solution)/shard_map/ppermute | solution.py:46
  81.5 4.1 %product.3 = bf16[16,2,2,3,64,128]{5,4,3,2,1,0:T(8,128)(2,1)} custom-call(bf16[2,3,32,1024]{3,2,1,0:T(8,128)(2,1)} %get-tuple-element.14.refs_0_, bf16[2,3,32,1024]{3,2,1,0:T(8,128)(2,1)} %copy-done.1, bf16[2,3,32,1024]{3,2,1,0:T(8,128)(2,1)} %copy-done.2, bf16[2,3,32,1024]{3,2,1,0:T(8,128)(2,1)} %collective-permute-done.7.refs_3_), custom_call_target="tpu_custom_call" | custom-call | flops 805306368 | bytes 6291456 | tf_op jit(solution)/shard_map/product/pallas_call | solution.py:310
  85.6 7.0 %all-to-all-start.2 = ((bf16[16,2,2,3,64,128]{5,4,3,2,1,0:T(8,128)(2,1)}), bf16[16,2,2,3,64,128]{5,4,3,2,1,0:T(8,128)(2,1)}, u32[]{:S(2)}, u32[]{:S(2)}) async-start(bf16[16,2,2,3,64,128]{5,4,3,2,1,0:T(8,128)(2,1)} %product.3), calls=%async_computation.2 | async-start | bytes 6291456 | tf_op jit(solution)/shard_map/all_to_all | solution.py:38
  92.5 2.1 %place.4.refs_0_ = bf16[2,160,64,128]{3,2,1,0:T(8,128)(2,1)} custom-call(bf16[16,2,2,2,64,128]{5,4,3,2,1,0:T(8,128)(2,1)} %all-to-all-done.1.in_ref), custom_call_target="tpu_custom_call" | custom-call | tf_op jit(solution)/shard_map/place/pallas_call | solution.py:363
  94.7 2.4 %collective-permute-done.4.in_ref = bf16[16,2,2,2,64,128]{5,4,3,2,1,0:T(8,128)(2,1)} collective-permute-done((bf16[16,2,2,2,64,128]{5,4,3,2,1,0:T(8,128)(2,1)}, bf16[16,2,2,2,64,128]{5,4,3,2,1,0:T(8,128)(2,1)}, u32[]{:S(2)}, u32[]{:S(2)}) %collective-permute-start.4) | collective-permute-done | bytes 2097184 | tf_op jit(solution)/shard_map/ppermute | solution.py:46
  97.0 2.1 %place.5.refs_0_ = bf16[2,160,64,128]{3,2,1,0:T(8,128)(2,1)} custom-call(bf16[16,2,2,2,64,128]{5,4,3,2,1,0:T(8,128)(2,1)} %collective-permute-done.4.in_ref, bf16[2,160,64,128]{3,2,1,0:T(8,128)(2,1)} %place.4.refs_0_), custom_call_target="tpu_custom_call", output_to_operand_aliasing={{}: (1, {})} | custom-call | tf_op jit(solution)/shard_map/place/pallas_call | solution.py:363
  99.2 30.3 %all-to-all-done.2.in_ref = bf16[16,2,2,3,64,128]{5,4,3,2,1,0:T(8,128)(2,1)} async-done(((bf16[16,2,2,3,64,128]{5,4,3,2,1,0:T(8,128)(2,1)}), bf16[16,2,2,3,64,128]{5,4,3,2,1,0:T(8,128)(2,1)}, u32[]{:S(2)}, u32[]{:S(2)}) %all-to-all-start.2) | async-done | bytes 3145760 | tf_op jit(solution)/shard_map/all_to_all | solution.py:38
  129.8 2.4 %place.6.refs_0_ = bf16[2,160,64,128]{3,2,1,0:T(8,128)(2,1)} custom-call(bf16[16,2,2,3,64,128]{5,4,3,2,1,0:T(8,128)(2,1)} %all-to-all-done.2.in_ref, bf16[2,160,64,128]{3,2,1,0:T(8,128)(2,1)} %place.5.refs_0_), custom_call_target="tpu_custom_call", output_to_operand_aliasing={{}: (1, {})} | custom-call | tf_op jit(solution)/shard_map/place/pallas_call | solution.py:363
  132.2 3.2 %collective-permute-done.8.in_ref = bf16[16,2,2,3,64,128]{5,4,3,2,1,0:T(8,128)(2,1)} collective-permute-done((bf16[16,2,2,3,64,128]{5,4,3,2,1,0:T(8,128)(2,1)}, bf16[16,2,2,3,64,128]{5,4,3,2,1,0:T(8,128)(2,1)}, u32[]{:S(2)}, u32[]{:S(2)}) %collective-permute-start.8) | collective-permute-done | bytes 3145760 | tf_op jit(solution)/shard_map/ppermute | solution.py:46
  135.5 2.4 %place.7 = bf16[2,160,64,128]{3,2,1,0:T(8,128)(2,1)} custom-call(bf16[16,2,2,3,64,128]{5,4,3,2,1,0:T(8,128)(2,1)} %collective-permute-done.8.in_ref, bf16[2,160,64,128]{3,2,1,0:T(8,128)(2,1)} %place.6.refs_0_), custom_call_target="tpu_custom_call", output_to_operand_aliasing={{}: (1, {})} | custom-call | tf_op jit(solution)/shard_map/place/pallas_call | solution.py:363
  (19 shorter events, 3.0 us)
Async XLA Ops:
  15.4 2.2 %collective-permute-start = (bf16[16,80,128]{2,1,0:T(8,128)(2,1)}, bf16[16,80,128]{2,1,0:T(8,128)(2,1)S(1)}, u32[]{:S(2)}, u32[]{:S(2)}) collective-permute-start(bf16[16,80,128]{2,1,0:T(8,128)(2,1)} %get-tuple-element.12), channel_id=1, source_target_pairs={{0,8},{8,0},{1,9},{9,1},{16,24},{24,16},{17,25},{25,17},{2,10},{10... | collective-permute-start | bytes 983048 | tf_op jit(solution)/shard_map/ppermute | solution.py:46
  38.6 18.8 %copy-start = (bf16[2,3,32,1024]{3,2,1,0:T(8,128)(2,1)S(1)}, bf16[2,3,32,1024]{3,2,1,0:T(8,128)(2,1)}, u32[]{:S(2)}) copy-start(bf16[2,3,32,1024]{3,2,1,0:T(8,128)(2,1)} %get-tuple-element.14.refs_0_) | copy-start | bytes 1179652
  38.6 5.7 %collective-permute-start.1 = (bf16[2,2,32,1024]{3,2,1,0:T(8,128)(2,1)}, bf16[2,2,32,1024]{3,2,1,0:T(8,128)(2,1)S(1)}, u32[]{:S(2)}, u32[]{:S(2)}) collective-permute-start(bf16[2,2,32,1024]{3,2,1,0:T(8,128)(2,1)} %get-tuple-element.13.refs_0_), channel_id=1, source_target_pairs={{0,2},{8,40},{1,3},{9,41},{16,18},{24,56},{17,19},{25,57},{2,4},{1... | collective-permute-start | bytes 786440 | tf_op jit(solution)/shard_map/ppermute | solution.py:46
  38.6 7.0 %collective-permute-start.2 = (bf16[2,2,32,1024]{3,2,1,0:T(8,128)(2,1)}, bf16[2,2,32,1024]{3,2,1,0:T(8,128)(2,1)S(1)}, u32[]{:S(2)}, u32[]{:S(2)}) collective-permute-start(bf16[2,2,32,1024]{3,2,1,0:T(8,128)(2,1)} %get-tuple-element.13.refs_0_), channel_id=1, source_target_pairs={{0,4},{8,72},{1,5},{9,73},{16,20},{24,88},{17,21},{25,89},{2,6},{1... | collective-permute-start | bytes 786440 | tf_op jit(solution)/shard_map/ppermute | solution.py:46
  41.0 7.5 %collective-permute-start.3 = (bf16[2,2,32,1024]{3,2,1,0:T(8,128)(2,1)}, bf16[2,2,32,1024]{3,2,1,0:T(8,128)(2,1)}, u32[]{:S(2)}, u32[]{:S(2)}) collective-permute-start(bf16[2,2,32,1024]{3,2,1,0:T(8,128)(2,1)} %get-tuple-element.13.refs_0_), channel_id=1, source_target_pairs={{0,6},{8,104},{1,7},{9,105},{16,22},{24,120},{17,23},{25,121},{2,0... | collective-permute-start | bytes 786440 | tf_op jit(solution)/shard_map/ppermute | solution.py:46
  44.4 4.2 %copy-start.3 = (bf16[2,2,32,1024]{3,2,1,0:T(8,128)(2,1)}, bf16[2,2,32,1024]{3,2,1,0:T(8,128)(2,1)S(1)}, u32[]{:S(2)}) copy-start(bf16[2,2,32,1024]{3,2,1,0:T(8,128)(2,1)S(1)} %collective-permute-done.1.refs_1_) | copy-start | bytes 786436
  45.6 2.9 %copy-start.4 = (bf16[2,2,32,1024]{3,2,1,0:T(8,128)(2,1)}, bf16[2,2,32,1024]{3,2,1,0:T(8,128)(2,1)S(1)}, u32[]{:S(2)}) copy-start(bf16[2,2,32,1024]{3,2,1,0:T(8,128)(2,1)S(1)} %collective-permute-done.2.refs_2_) | copy-start | bytes 786436
  51.7 33.8 %all-to-all-start.1 = ((bf16[16,2,2,2,64,128]{5,4,3,2,1,0:T(8,128)(2,1)}), bf16[16,2,2,2,64,128]{5,4,3,2,1,0:T(8,128)(2,1)}, u32[]{:S(2)}, u32[]{:S(2)}) async-start(bf16[16,2,2,2,64,128]{5,4,3,2,1,0:T(8,128)(2,1)} %product.2), calls=%async_computation.1 | async-start | bytes 4194304 | tf_op jit(solution)/shard_map/all_to_all | solution.py:38
  57.5 8.1 %collective-permute-start.5 = (bf16[2,3,32,1024]{3,2,1,0:T(8,128)(2,1)S(1)}, bf16[2,3,32,1024]{3,2,1,0:T(8,128)(2,1)S(1)}, u32[]{:S(2)}, u32[]{:S(2)}) collective-permute-start(bf16[2,3,32,1024]{3,2,1,0:T(8,128)(2,1)S(1)} %copy-done), channel_id=1, source_target_pairs={{0,2},{8,40},{1,3},{9,41},{16,18},{24,56},{17,19},{25,57},{2,4},{1... | collective-permute-start | bytes 1179656 | tf_op jit(solution)/shard_map/ppermute | solution.py:46
  58.7 11.8 %collective-permute-start.6 = (bf16[2,3,32,1024]{3,2,1,0:T(8,128)(2,1)S(1)}, bf16[2,3,32,1024]{3,2,1,0:T(8,128)(2,1)S(1)}, u32[]{:S(2)}, u32[]{:S(2)}) collective-permute-start(bf16[2,3,32,1024]{3,2,1,0:T(8,128)(2,1)S(1)} %copy-done), channel_id=1, source_target_pairs={{0,4},{8,72},{1,5},{9,73},{16,20},{24,88},{17,21},{25,89},{2,6},{1... | collective-permute-start | bytes 1179656 | tf_op jit(solution)/shard_map/ppermute | solution.py:46
  60.2 21.3 %collective-permute-start.7 = (bf16[2,3,32,1024]{3,2,1,0:T(8,128)(2,1)S(1)}, bf16[2,3,32,1024]{3,2,1,0:T(8,128)(2,1)}, u32[]{:S(2)}, u32[]{:S(2)}) collective-permute-start(bf16[2,3,32,1024]{3,2,1,0:T(8,128)(2,1)S(1)} %copy-done), channel_id=1, source_target_pairs={{0,6},{8,104},{1,7},{9,105},{16,22},{24,120},{17,23},{25,121},{2,0... | collective-permute-start | bytes 1179656 | tf_op jit(solution)/shard_map/ppermute | solution.py:46
  65.6 15.9 %copy-start.1 = (bf16[2,3,32,1024]{3,2,1,0:T(8,128)(2,1)}, bf16[2,3,32,1024]{3,2,1,0:T(8,128)(2,1)S(1)}, u32[]{:S(2)}) copy-start(bf16[2,3,32,1024]{3,2,1,0:T(8,128)(2,1)S(1)} %collective-permute-done.5.refs_1_) | copy-start | bytes 1179652
  70.5 0.7 copy-start.2
  85.6 43.9 %all-to-all-start.2 = ((bf16[16,2,2,3,64,128]{5,4,3,2,1,0:T(8,128)(2,1)}), bf16[16,2,2,3,64,128]{5,4,3,2,1,0:T(8,128)(2,1)}, u32[]{:S(2)}, u32[]{:S(2)}) async-start(bf16[16,2,2,3,64,128]{5,4,3,2,1,0:T(8,128)(2,1)} %product.3), calls=%async_computation.2 | async-start | bytes 6291456 | tf_op jit(solution)/shard_map/all_to_all | solution.py:38
  92.5 4.5 %collective-permute-start.4 = (bf16[16,2,2,2,64,128]{5,4,3,2,1,0:T(8,128)(2,1)}, bf16[16,2,2,2,64,128]{5,4,3,2,1,0:T(8,128)(2,1)}, u32[]{:S(2)}, u32[]{:S(2)}) collective-permute-start(bf16[16,2,2,2,64,128]{5,4,3,2,1,0:T(8,128)(2,1)} %all-to-all-done.1.in_ref), channel_id=1, source_target_pairs={{0,8},{8,0},{1,9},{9,1},{16,24},{24,16},{17,25},{25,17},{2,10},{10... | collective-permute-start | bytes 6291464 | tf_op jit(solution)/shard_map/ppermute | solution.py:46
  129.5 6.0 %collective-permute-start.8 = (bf16[16,2,2,3,64,128]{5,4,3,2,1,0:T(8,128)(2,1)}, bf16[16,2,2,3,64,128]{5,4,3,2,1,0:T(8,128)(2,1)}, u32[]{:S(2)}, u32[]{:S(2)}) collective-permute-start(bf16[16,2,2,3,64,128]{5,4,3,2,1,0:T(8,128)(2,1)} %all-to-all-done.2.in_ref), channel_id=1, source_target_pairs={{0,8},{8,0},{1,9},{9,1},{16,24},{24,16},{17,25},{25,17},{2,10},{10... | collective-permute-start | bytes 9437192 | tf_op jit(solution)/shard_map/ppermute | solution.py:46
